TPU v7x, 32 devices: a whole 2x2x4 slice. The times are simulated.
32 devices in a mesh: expert: 8 (over z, y), group: 4 (over x, core).
Axes of the slice: x: 2, y: 2, z: 4, core: 2. Of those that a mesh axis runs over, the one named last changes fastest.
Arguments:
- tokens: bfloat16 [4096, 1024], P(('expert', 'group')), may hold values from -6 to 6
- out_grad: bfloat16 [4096, 1024], P(('expert', 'group')), may hold values from -6 to 6
- w_router: bfloat16 [1024, 256], P('group', 'expert'), may hold values from -0.1875 to 0.1875
- w_in: bfloat16 [8, 1024, 2048], P('expert', None, 'group'), may hold values from -0.1875 to 0.1875
- w_out: bfloat16 [8, 2048, 1024], P('expert', 'group'), may hold values from -0.09375 to 0.09375
- expert_ids: int32 [4096, 2], P(('expert', 'group')), may hold values from 0 to 255, as said below
- slot_ids: int32 [4096, 2], P(('expert', 'group')), may hold values from 0 to 1, as said below
- keep_mask: int32 [4096, 2], P(('expert', 'group')), may hold values 0 or 1
Outputs:
- in_grad: bfloat16 [4096, 1024], P(('expert', 'group'))
- w_in_grad: bfloat16 [8, 1024, 2048], P('expert', None, 'group')
- w_out_grad: bfloat16 [8, 2048, 1024], P('expert', 'group')
- router_grad: float32 [1024, 256], P('group', 'expert')
Inputs may be any that keep to these rules, and one draw needn't show every extreme that they name: `expert_ids`: the two ids of a token differ. Among the tokens of one device no expert is named more than 2 times, and in every draw some expert below 4 is named 2 times by the tokens of every device. slot_ids[t, 0] is 0; slot_ids[t, 1] is 1 exactly when the second expert of token t is also the first expert of another token of the same device, else 0; so on one device no two choices share both expert and slot.
All inputs are finite; a program needn't handle non-finite values. No bound on the sum of `keep_mask` on one device may be relied on, other than what follows from the above.
Results may differ from a plain program's by a relative error of at most 0.015.
Values may be sent and summed in bfloat16 or wider, within the bound.
A program may use at most 64 MiB of HBM per device.

v0:
```python
import jax
import jax.numpy as jnp
from jax import lax
from jax.sharding import PartitionSpec as P

CAP = 2
SPLIT = 2


def gelu_parts(pre_act):
    cubic_term = 0.044715 * pre_act * pre_act * pre_act
    tanh_value = jnp.tanh(0.7978845608028654 * (pre_act + cubic_term))
    gelu_value = 0.5 * pre_act * (1.0 + tanh_value)
    gelu_slope = 0.5 * (1.0 + tanh_value) + 0.5 * pre_act * (
        1.0 - tanh_value * tanh_value
    ) * 0.7978845608028654 * (1.0 + 3.0 * 0.044715 * pre_act * pre_act)
    return (gelu_value, gelu_slope)


def expert_rows(w_in_local, w_out_local, pieces):
    x_piece, dy_piece, gate_piece = pieces
    gate_col = gate_piece.astype(jnp.float32)[:, None]
    pre_act = jnp.dot(x_piece, w_in_local, preferred_element_type=jnp.float32)
    gelu_value, gelu_slope = gelu_parts(pre_act)
    back_up = jnp.einsum("rd,hd->rh", dy_piece, w_out_local, preferred_element_type=jnp.float32)
    gate_piece_sum = jnp.sum(back_up * gelu_value, axis=1)
    pre_grad = (gate_col * back_up * gelu_slope).astype(jnp.bfloat16)
    scaled_grad = (gate_col * dy_piece.astype(jnp.float32)).astype(jnp.bfloat16)
    sum_in = jnp.einsum("rd,rh->dh", x_piece, pre_grad, preferred_element_type=jnp.float32)
    sum_out = jnp.einsum(
        "rh,rd->hd",
        gelu_value.astype(jnp.bfloat16),
        scaled_grad,
        preferred_element_type=jnp.float32,
    )
    part_rows = jnp.einsum("rh,dh->rd", pre_grad, w_in_local, preferred_element_type=jnp.float32)
    return (sum_in, sum_out, part_rows, gate_piece_sum)


def body(tokens, out_grad, w_router, w_in, w_out, expert_ids, slot_ids, keep_mask):
    expert_count = lax.axis_size("expert")
    window = expert_count // SPLIT
    slot_count = window * CAP
    model_width = tokens.shape[1]
    router_full = lax.all_gather(
        lax.all_gather(w_router, "expert", axis=1, tiled=True), "group", axis=0, tiled=True
    )
    logits = jnp.dot(tokens, router_full, preferred_element_type=jnp.float32)
    uniform_samples = jnp.arange(router_full.shape[1], dtype=jnp.int32)
    first_hot = (expert_ids[:, 0:1] == uniform_samples[None, :]).astype(jnp.float32)
    second_hot = (expert_ids[:, 1:2] == uniform_samples[None, :]).astype(jnp.float32)
    logit_gap = jnp.sum(logits * first_hot, axis=1) - jnp.sum(logits * second_hot, axis=1)
    combine = jnp.stack([jax.nn.sigmoid(logit_gap), jax.nn.sigmoid(-logit_gap)], axis=1)
    active = (keep_mask == 1) & (expert_ids < window)
    slot_code = jnp.where(active, expert_ids * CAP + slot_ids, -1)
    slot_axis = jnp.arange(slot_count, dtype=jnp.int32)
    place_first = (slot_code[:, 0:1] == slot_axis[None, :]).astype(jnp.float32)
    place_second = (slot_code[:, 1:2] == slot_axis[None, :]).astype(jnp.float32)
    placement = place_first + place_second
    place_round = placement.astype(jnp.bfloat16)
    token_slots = jnp.einsum(
        "ts,td->sd", place_round, tokens, preferred_element_type=jnp.float32
    ).astype(jnp.bfloat16)
    grad_slots = jnp.einsum(
        "ts,td->sd", place_round, out_grad, preferred_element_type=jnp.float32
    ).astype(jnp.bfloat16)
    gate_slots = jnp.sum(
        place_first * combine[:, 0:1] + place_second * combine[:, 1:2], axis=0
    ).astype(jnp.bfloat16)
    token_send = jnp.repeat(token_slots.reshape(window, CAP, model_width), SPLIT, axis=0)
    grad_send = jnp.repeat(grad_slots.reshape(window, CAP, model_width), SPLIT, axis=0)
    gate_send = jnp.repeat(gate_slots.reshape(window, CAP), SPLIT, axis=0)
    token_recv, grad_recv, gate_recv = (
        lax.all_to_all(token_send, "expert", split_axis=0, concat_axis=0, tiled=True),
        lax.all_to_all(grad_send, "expert", split_axis=0, concat_axis=0, tiled=True),
        lax.all_to_all(gate_send, "expert", split_axis=0, concat_axis=0, tiled=True),
    )
    row_count = expert_count * CAP
    token_rows = token_recv.reshape(row_count, model_width)
    grad_rows = grad_recv.reshape(row_count, model_width)
    gate_rows = gate_recv.reshape(row_count)
    w_in_local = w_in[0]
    w_out_local = w_out[0]
    sum_in, sum_out, row_parts, gate_parts = expert_rows(
        w_in_local,
        w_out_local,
        (
            lax.all_gather(token_rows, "group", axis=0, tiled=True),
            lax.all_gather(grad_rows, "group", axis=0, tiled=True),
            lax.all_gather(gate_rows, "group", axis=0, tiled=True),
        ),
    )
    w_in_grad = sum_in.astype(jnp.bfloat16)[None]
    w_out_grad = sum_out.astype(jnp.bfloat16)[None]
    row_sums = lax.psum_scatter(
        row_parts.astype(jnp.bfloat16), "group", scatter_dimension=0, tiled=True
    ).astype(jnp.float32)
    gate_sums = lax.psum_scatter(gate_parts, "group", scatter_dimension=0, tiled=True)
    rows_back, gates_back = (
        lax.all_to_all(
            row_sums.reshape(expert_count, CAP, model_width).astype(jnp.bfloat16),
            "expert",
            split_axis=0,
            concat_axis=0,
            tiled=True,
        ).astype(jnp.float32),
        lax.all_to_all(
            gate_sums.reshape(expert_count, CAP).astype(jnp.bfloat16),
            "expert",
            split_axis=0,
            concat_axis=0,
            tiled=True,
        ).astype(jnp.float32),
    )
    rows_back = jnp.sum(rows_back.reshape(window, SPLIT, CAP, model_width), axis=1).reshape(
        slot_count, model_width
    )
    gates_back = jnp.sum(gates_back.reshape(window, SPLIT, CAP), axis=1).reshape(slot_count)
    expert_part = jnp.dot(placement, rows_back, precision=lax.Precision.HIGHEST)
    gate_first = jnp.sum(place_first * gates_back[None, :], axis=1)
    gate_second = jnp.sum(place_second * gates_back[None, :], axis=1)
    gate_slope = combine[:, 0] * combine[:, 1] * (gate_first - gate_second)
    logit_grad = first_hot * gate_slope[:, None] - second_hot * gate_slope[:, None]
    router_part = jnp.dot(
        logit_grad, router_full.astype(jnp.float32).T, precision=lax.Precision.HIGHEST
    )
    in_grad = (expert_part + router_part).astype(jnp.bfloat16)
    router_sum = jnp.dot(tokens.astype(jnp.float32).T, logit_grad, precision=lax.Precision.HIGHEST)
    router_grad = lax.psum_scatter(
        lax.psum_scatter(router_sum, "expert", scatter_dimension=1, tiled=True),
        "group",
        scatter_dimension=0,
        tiled=True,
    )
    return (in_grad, w_in_grad, w_out_grad, router_grad)


def solution(mesh):
    return jax.shard_map(
        body,
        mesh=mesh,
        in_specs=(
            P(("expert", "group"), None),
            P(("expert", "group"), None),
            P("group", "expert"),
            P("expert", None, "group"),
            P("expert", "group", None),
            P(("expert", "group"), None),
            P(("expert", "group"), None),
            P(("expert", "group"), None),
        ),
        out_specs=(
            P(("expert", "group"), None),
            P("expert", None, "group"),
            P("expert", "group", None),
            P("group", "expert"),
        ),
        check_vma=False,
    )
```

profile of v0, /device:TPU:0, one launch (start us, length us, event | category | flops | bytes accessed | tf_op | source)
XLA Modules:
  0.0 227.5 jit_solution(16638587368337232546)
XLA Ops:
  7.2 0.8 and_select_fusion
  8.0 1.1 convolution_convert_fusion.3
  9.1 0.6 broadcast_in_dim.29
  9.8 7.3 %all-to-all-start.2 = ((bf16[8,2,1024]{2,1,0:T(2,128)(2,1)}), bf16[8,2,1024]{2,1,0:T(2,128)(2,1)S(1)}, u32[]{:S(2)}, u32[]{:S(2)}) async-start(bf16[8,2,1024]{2,1,0:T(2,128)(2,1)} %bitcast.7), calls=%async_computation.2 | async-start | bytes 65536 | tf_op jit(solution)/shard_map/all_to_all | solution.py:74
  17.1 0.8 slice_bitcast_fusion.1
  17.8 1.1 convolution_convert_fusion.4
  18.9 31.3 %all_gather.15 = bf16[256,256]{0,1:T(8,128)(2,1)S(1)} all-gather(bf16[256,32]{0,1:T(8,128)(2,1)} %param.10), channel_id=1, replica_groups=mesh['expert'=8,'group'=4] {'expert'}, dimensions={1}, use_global_device_ids=true | all-gather | bytes 147456 | tf_op jit(solution)/shard_map/all_gather | solution.py:46
  50.2 7.2 %all_gather.16 = bf16[1024,256]{0,1:T(8,128)(2,1)S(1)} all-gather(bf16[256,256]{0,1:T(8,128)(2,1)S(1)} %all_gather.15), channel_id=1, replica_groups=mesh['expert'=8,'group'=4] {'group'}, dimensions={0}, use_global_device_ids=true | all-gather | bytes 655360 | tf_op jit(solution)/shard_map/all_gather | solution.py:45
  57.4 0.6 broadcast_in_dim.28
  58.0 5.5 %all-to-all-start.1 = ((bf16[8,2,1024]{2,1,0:T(2,128)(2,1)}), bf16[8,2,1024]{2,1,0:T(2,128)(2,1)S(1)}, u32[]{:S(2)}, u32[]{:S(2)}) async-start(bf16[8,2,1024]{2,1,0:T(2,128)(2,1)} %bitcast.5), calls=%async_computation.1 | async-start | bytes 65536 | tf_op jit(solution)/shard_map/all_to_all | solution.py:75
  63.9 0.6 fusion.41
  65.2 5.4 %all_gather.19 = bf16[64,1024]{1,0:T(8,128)(2,1)S(1)} all-gather(bf16[16,1024]{1,0:T(8,128)(2,1)S(1)} %reshape.101), channel_id=1, replica_groups=mesh['expert'=8,'group'=4] {'group'}, dimensions={0}, use_global_device_ids=true | all-gather | bytes 163840 | tf_op jit(solution)/shard_map/all_gather | solution.py:88
  70.7 5.4 %all_gather.18 = bf16[64,1024]{1,0:T(8,128)(2,1)S(1)} all-gather(bf16[16,1024]{1,0:T(8,128)(2,1)S(1)} %reshape.98), channel_id=1, replica_groups=mesh['expert'=8,'group'=4] {'group'}, dimensions={0}, use_global_device_ids=true | all-gather | bytes 163840 | tf_op jit(solution)/shard_map/all_gather | solution.py:89
  76.4 0.5 multiply_reduce_fusion
  76.9 6.4 %all-reduce.1 = bf16[64]{0:T(256)(128)(2,1)S(1)} all-reduce(f32[64]{0:T(128)S(1)} %get-tuple-element.17), channel_id=3, replica_groups=mesh['expert'=8,'group'=4] {'group'}, use_global_device_ids=true, to_apply=%region_6.7.clone | all-reduce | flops 64 | bytes 384
  83.5 0.7 convert_element_type.105
  84.2 6.0 %all-to-all-start.4 = ((bf16[8,1,2]{2,1,0:T(2,128)(2,1)}), bf16[8,1,2]{2,1,0:T(2,128)(2,1)S(1)}, u32[]{:S(2)}, u32[]{:S(2)}) async-start(bf16[8,1,2]{2,1,0:T(2,128)(2,1)} %convert_element_type.105), calls=%async_computation.5 | async-start | bytes 8192 | tf_op jit(solution)/shard_map/all_to_all | solution.py:107
  90.2 6.4 %all-to-all-done.4 = bf16[8,1,2]{2,1,0:T(2,128)(2,1)S(1)} async-done(((bf16[8,1,2]{2,1,0:T(2,128)(2,1)}), bf16[8,1,2]{2,1,0:T(2,128)(2,1)S(1)}, u32[]{:S(2)}, u32[]{:S(2)}) %all-to-all-start.4) | async-done | bytes 64 | tf_op jit(solution)/shard_map/all_to_all | solution.py:107
  97.5 0.7 copy.29
  98.2 3.3 %all-to-all-start = ((bf16[8,1,2]{2,1,0:T(2,128)(2,1)}), bf16[8,1,2]{2,1,0:T(2,128)(2,1)S(1)}, u32[]{:S(2)}, u32[]{:S(2)}) async-start(bf16[8,1,2]{2,1,0:T(2,128)(2,1)} %copy.29), calls=%async_computation | async-start | bytes 8192 | tf_op jit(solution)/shard_map/all_to_all | solution.py:76
  102.2 5.6 %all-to-all-done = bf16[8,1,2]{2,1,0:T(2,128)(2,1)S(1)} async-done(((bf16[8,1,2]{2,1,0:T(2,128)(2,1)}), bf16[8,1,2]{2,1,0:T(2,128)(2,1)S(1)}, u32[]{:S(2)}, u32[]{:S(2)}) %all-to-all-start) | async-done | bytes 64 | tf_op jit(solution)/shard_map/all_to_all | solution.py:76
  108.2 5.6 %all-reduce = bf16[64]{0:T(256)(128)(2,1)S(1)} all-reduce(bf16[64]{0:T(256)(128)(2,1)S(1)} %dynamic-update-slice), channel_id=1, replica_groups=mesh['expert'=8,'group'=4] {'group'}, use_global_device_ids=true, to_apply=%add | all-reduce | flops 64 | bytes 256
  113.8 1.1 convolution_convert_fusion.2
  115.0 1.7 convolution_bitcast_fusion
  117.2 1.5 fusion
  118.7 13.0 %reduce-scatter.4.cloned.1.call-done = bf16[16,1024]{1,0:T(8,128)(2,1)} async-done(((bf16[64,1024]{1,0:T(8,128)(2,1)}), bf16[16,1024]{1,0:T(8,128)(2,1)}) %reduce-scatter.4.cloned.1.call-update) | async-done | bytes 32784 | tf_op jit(solution)/shard_map/reduce_scatter | solution.py:95
  131.7 1.4 convert_element_type.93
  133.1 5.5 %all-to-all-start.3 = ((bf16[8,2,1024]{2,1,0:T(2,128)(2,1)}), bf16[8,2,1024]{2,1,0:T(2,128)(2,1)S(1)}, u32[]{:S(2)}, u32[]{:S(2)}) async-start(bf16[8,2,1024]{2,1,0:T(2,128)(2,1)} %convert_element_type.93), calls=%async_computation.4 | async-start | bytes 65536 | tf_op jit(solution)/shard_map/all_to_all | solution.py:100
  138.6 1.5 fusion.1
  140.1 59.2 %reduce-scatter.6.cloned.1.call-done = f32[1024,32]{0,1:T(8,128)} async-done(((f32[1024,256]{0,1:T(8,128)}), f32[1024,32]{0,1:T(8,128)}) %reduce-scatter.6.cloned.1.call-update) | async-done | bytes 131088 | tf_op jit(solution)/shard_map/reduce_scatter | solution.py:130
  199.4 1.3 fusion.2
  200.7 20.2 %reduce-scatter.8.cloned.1.call-done = f32[256,32]{0,1:T(8,128)} async-done(((f32[1024,32]{0,1:T(8,128)}), f32[256,32]{0,1:T(8,128)}) %reduce-scatter.8.cloned.1.call-update) | async-done | bytes 32784 | tf_op jit(solution)/shard_map/reduce_scatter | solution.py:129
  (45 shorter events, 2.8 us)
Async XLA Ops:
  7.2 68.9 %copy-start = (bf16[1,1024,512]{2,1,0:T(8,128)(2,1)S(1)}, bf16[1,1024,512]{2,1,0:T(8,128)(2,1)}, u32[]{:S(2)}) copy-start(bf16[1,1024,512]{2,1,0:T(8,128)(2,1)} %param.11) | copy-start | bytes 3145732
  7.2 56.3 %copy-start.2 = (bf16[128,1024]{1,0:T(8,128)(2,1)S(1)}, bf16[128,1024]{1,0:T(8,128)(2,1)}, u32[]{:S(2)}) copy-start(bf16[128,1024]{1,0:T(8,128)(2,1)} %param.8) | copy-start | bytes 786436
  9.8 47.6 %all-to-all-start.2 = ((bf16[8,2,1024]{2,1,0:T(2,128)(2,1)}), bf16[8,2,1024]{2,1,0:T(2,128)(2,1)S(1)}, u32[]{:S(2)}, u32[]{:S(2)}) async-start(bf16[8,2,1024]{2,1,0:T(2,128)(2,1)} %bitcast.7), calls=%async_computation.2 | async-start | bytes 65536 | tf_op jit(solution)/shard_map/all_to_all | solution.py:74
  17.8 46.1 %copy-start.3 = (u32[32]{0:T(128)S(1)}, u32[32]{0:T(128)}, u32[]{:S(2)}) copy-start(u32[32]{0:T(128)} %constant.33) | copy-start | bytes 388
  58.0 12.6 %all-to-all-start.1 = ((bf16[8,2,1024]{2,1,0:T(2,128)(2,1)}), bf16[8,2,1024]{2,1,0:T(2,128)(2,1)S(1)}, u32[]{:S(2)}, u32[]{:S(2)}) async-start(bf16[8,2,1024]{2,1,0:T(2,128)(2,1)} %bitcast.5), calls=%async_computation.1 | async-start | bytes 65536 | tf_op jit(solution)/shard_map/all_to_all | solution.py:75
  63.9 12.5 %copy-start.1 = (bf16[1,512,1024]{2,1,0:T(8,128)(2,1)S(1)}, bf16[1,512,1024]{2,1,0:T(8,128)(2,1)}, u32[]{:S(2)}) copy-start(bf16[1,512,1024]{2,1,0:T(8,128)(2,1)} %param.12) | copy-start | bytes 3145732
  84.2 12.4 %all-to-all-start.4 = ((bf16[8,1,2]{2,1,0:T(2,128)(2,1)}), bf16[8,1,2]{2,1,0:T(2,128)(2,1)S(1)}, u32[]{:S(2)}, u32[]{:S(2)}) async-start(bf16[8,1,2]{2,1,0:T(2,128)(2,1)} %convert_element_type.105), calls=%async_computation.5 | async-start | bytes 8192 | tf_op jit(solution)/shard_map/all_to_all | solution.py:107
  98.2 9.6 %all-to-all-start = ((bf16[8,1,2]{2,1,0:T(2,128)(2,1)}), bf16[8,1,2]{2,1,0:T(2,128)(2,1)S(1)}, u32[]{:S(2)}, u32[]{:S(2)}) async-start(bf16[8,1,2]{2,1,0:T(2,128)(2,1)} %copy.29), calls=%async_computation | async-start | bytes 8192 | tf_op jit(solution)/shard_map/all_to_all | solution.py:76
  101.5 30.2 %reduce-scatter.4.cloned.1.call-start = ((), (), s32[]{:S(2)}) async-start(), calls=%async_computation.8 | async-start | bytes 163840 | tf_op jit(solution)/shard_map/reduce_scatter | solution.py:95
  115.0 84.3 %reduce-scatter.6.cloned.1.call-start = ((), (), s32[]{:S(2)}) async-start(), calls=%async_computation.9 | async-start | bytes 1179648 | tf_op jit(solution)/shard_map/reduce_scatter | solution.py:130
  133.1 66.3 %all-to-all-start.3 = ((bf16[8,2,1024]{2,1,0:T(2,128)(2,1)}), bf16[8,2,1024]{2,1,0:T(2,128)(2,1)S(1)}, u32[]{:S(2)}, u32[]{:S(2)}) async-start(bf16[8,2,1024]{2,1,0:T(2,128)(2,1)} %convert_element_type.93), calls=%async_computation.4 | async-start | bytes 65536 | tf_op jit(solution)/shard_map/all_to_all | solution.py:100
  138.6 82.4 %reduce-scatter.8.cloned.1.call-start = ((), (), s32[]{:S(2)}) async-start(), calls=%async_computation.10 | async-start | bytes 163840 | tf_op jit(solution)/shard_map/reduce_scatter | solution.py:129
Sparse Core Ops, SparseCore 0:
  115.1 16.5 reduce-scatter.3
  135.5 63.7 reduce-scatter.5
  202.3 18.5 reduce-scatter.7
where the time goes:
time: 228 us; the launch traced here: 227 us
  waiting for transfers between devices  104 us (46%)
  blocking collectives  61.4 us (27%)
  starting transfers between devices  27.7 us (12%)
  between operations  15.2 us (7%)
  matrix products  10.9 us (5%)
  local copies, waits for them, and re-layouts  6.66 us (3%)
    reduce_scatter x1, waiting for transfers between devices, body(): lax.psum_scatter(router_sum, 'expert', scatter_dimension=1, tiled=True)  59.2 us
    all_gather x1, blocking collectives, body(): lax.all_gather(w_router, 'expert', axis=1, tiled=True)  31.3 us
    reduce_scatter x1, waiting for transfers between devices, body(): lax.psum_scatter(lax.psum_scatter(router_sum, 'expert', scatter_dimension...  20.2 us
    reduce_scatter x1, waiting for transfers between devices, body(): lax.psum_scatter(row_parts.astype(jnp.bfloat16), 'group', scatter_dimensi...  13 us
    unnamed x2, blocking collectives  12.1 us
    all_to_all x1, starting transfers between devices, body(): lax.all_to_all(token_send, 'expert', split_axis=0, concat_axis=0, tiled=T...  7.28 us
    all_gather x1, blocking collectives, body(): lax.all_gather(lax.all_gather(w_router, 'expert', axis=1, tiled=True), 'g...  7.16 us
    all_to_all x1, waiting for transfers between devices, body(): lax.all_to_all(gate_sums.reshape(expert_count, CAP).astype(jnp.bfloat16),...  6.38 us
  transfers between devices with their start and end apart: 8, of which 5 were waited for; matrix products, arithmetic and copies ran while one was open for 5% of the time, Pallas kernels for 0%

commit v1 on v0

--- a/solution.py
+++ b/solution.py
@@ -1,10 +1,18 @@
+import functools
+
 import jax
 import jax.numpy as jnp
 from jax import lax
+from jax.experimental import pallas as pl
+from jax.experimental.pallas import tpu as pltpu
 from jax.sharding import PartitionSpec as P
 
 CAP = 2
 SPLIT = 2
+LANES = 128
+F32 = jnp.float32
+BF16 = jnp.bfloat16
+MESH = pl.DeviceIdType.MESH
 
 
 def gelu_parts(pre_act):
@@ -37,7 +45,7 @@
     return (sum_in, sum_out, part_rows, gate_piece_sum)
 
 
-def body(tokens, out_grad, w_router, w_in, w_out, expert_ids, slot_ids, keep_mask):
+def gathered_body(tokens, out_grad, w_router, w_in, w_out, expert_ids, slot_ids, keep_mask):
     expert_count = lax.axis_size("expert")
     window = expert_count // SPLIT
     slot_count = window * CAP
@@ -135,6 +143,429 @@
     return (in_grad, w_in_grad, w_out_grad, router_grad)
 
 
+def iota(shape, axis):
+    return lax.broadcasted_iota(jnp.int32, shape, axis)
+
+
+def one_hot(mask):
+    return jnp.where(mask, 1.0, 0.0).astype(F32)
+
+
+def contract(left, right, left_axis, right_axis):
+    return lax.dot_general(
+        left, right, (((left_axis,), (right_axis,)), ((), ())), preferred_element_type=F32
+    )
+
+
+def fused_kernel(
+    window,
+    groups,
+    tokens_hbm,
+    out_grad_hbm,
+    router_ref,
+    w_in_hbm,
+    w_out_hbm,
+    ids_ref,
+    slots_ref,
+    keep_ref,
+    in_grad_ref,
+    w_in_grad_hbm,
+    w_out_grad_hbm,
+    router_grad_ref,
+    tok,
+    outg,
+    w1,
+    w2,
+    g1,
+    g2,
+    z_send,
+    z_recv,
+    w_recv,
+    pack,
+    xs,
+    gv_send,
+    gv_recv,
+    gg,
+    rp_send,
+    rp_recv,
+    coef_ref,
+    rg_send,
+    rg_recv,
+    ret_send,
+    ret_recv,
+    load_sems,
+    store_sems,
+    zs,
+    zr,
+    ws,
+    wr,
+    pks,
+    pkr,
+    gvs,
+    gvr,
+    ggs,
+    ggr,
+    rps,
+    rpr,
+    rgs,
+    rgr,
+    rts,
+    rtr,
+):
+    plane = SPLIT * groups
+    width = tok.shape[1]
+    chunks = width // LANES
+    rows = window * CAP
+    message = z_send.shape[1]
+    used = CAP * (2 * chunks + 1)
+    columns, depth = router_ref.shape
+    ix = lax.axis_index("expert")
+    g = lax.axis_index("group")
+    z = ix // SPLIT
+    y = lax.rem(ix, SPLIT)
+    q = y * groups + g
+
+    def z_up(d):
+        return (lax.rem(z + d, window) * SPLIT + y, g)
+
+    def z_down(d):
+        return (lax.rem(z + window - d, window) * SPLIT + y, g)
+
+    def in_plane(p):
+        return (z * SPLIT + p // groups, lax.rem(p, groups))
+
+    def q_up(d):
+        return lax.rem(q + d, plane)
+
+    def q_down(d):
+        return lax.rem(q + plane - d, plane)
+
+    def remote(src, dst, send_sems, recv_sems, d, target):
+        return pltpu.make_async_remote_copy(
+            src_ref=src,
+            dst_ref=dst,
+            send_sem=send_sems.at[d],
+            recv_sem=recv_sems.at[d],
+            device_id=target,
+            device_id_type=MESH,
+        )
+
+    loads = [
+        pltpu.make_async_copy(src, dst, load_sems.at[i])
+        for i, (src, dst) in enumerate(
+            [
+                (tokens_hbm, tok),
+                (out_grad_hbm, outg),
+                (w_in_hbm.at[0], w1),
+                (w_out_hbm.at[0], w2),
+            ]
+        )
+    ]
+    for load in loads:
+        load.start()
+
+    barrier = pltpu.get_barrier_semaphore()
+    for d in range(1, window):
+        pl.semaphore_signal(barrier, inc=1, device_id=z_up(d), device_id_type=MESH)
+    for d in range(1, plane):
+        pl.semaphore_signal(barrier, inc=1, device_id=in_plane(q_up(d)), device_id_type=MESH)
+
+    places = []
+    for k in range(2):
+        ids = ids_ref[k : k + 1, :]
+        relative = jnp.where(ids < z, ids - z + window, ids - z)
+        active = (keep_ref[k : k + 1, :] == 1) & (ids < window)
+        code = jnp.where(active, relative * CAP + slots_ref[k : k + 1, :], -1)
+        places.append(one_hot(iota((LANES, LANES), 0) == code))
+    place = places[0] + places[1]
+    place_rows = place[:16].astype(BF16)
+    short = place[:rows]
+    first_id = jnp.sum(short * ids_ref[0:1, :].astype(F32), axis=1, keepdims=True)
+    second_id = jnp.sum(short * ids_ref[1:2, :].astype(F32), axis=1, keepdims=True)
+    which = jnp.sum(places[0][:rows] - places[1][:rows], axis=1, keepdims=True)
+    lane = iota((rows, LANES), 1)
+    meta = jnp.where(
+        lane == 0, first_id, jnp.where(lane == 1, second_id, jnp.where(lane == 2, which, 0.0))
+    )
+
+    loads[0].wait()
+    loads[1].wait()
+    x_slots = contract(place_rows, tok[...], 1, 0)[:rows]
+    dy_slots = contract(place_rows, outg[...], 1, 0)[:rows]
+    pieces = [x_slots[:, c * LANES : (c + 1) * LANES] for c in range(chunks)]
+    pieces += [dy_slots[:, c * LANES : (c + 1) * LANES] for c in range(chunks)]
+    pieces += [meta, jnp.zeros((rows, LANES), F32)]
+    folded = jnp.concatenate(pieces, axis=0).astype(BF16)
+    depth_f = folded.shape[0]
+    spread = []
+    for d in range(window):
+        row = iota((message, depth_f), 0)
+        source = (row >> 1) * rows + d * CAP + (row & 1)
+        spread.append(one_hot((iota((message, depth_f), 1) == source) & (row < used)))
+    messages = contract(jnp.concatenate(spread, axis=0).astype(BF16), folded, 1, 0).astype(BF16)
+    z_recv[0] = messages[:message]
+    for d in range(1, window):
+        z_send[d] = messages[d * message : (d + 1) * message]
+    w_recv[0] = router_ref[...]
+
+    pl.semaphore_wait(barrier, window - 1 + plane - 1)
+
+    z_copies, w_copies = [], []
+    for d in range(1, window):
+        z_copies.append(remote(z_send.at[d], z_recv.at[d], zs, zr, d, z_up(d)))
+        z_copies[-1].start()
+    for d in range(1, window):
+        w_copies.append(remote(router_ref, w_recv.at[d], ws, wr, d, z_up(d)))
+        w_copies[-1].start()
+
+    wide = (chunks + 1) * 16
+    row = iota((wide, window * message), 0)
+    inner = row & 15
+    chunk = row >> 4
+    block = jnp.where((inner < rows) & (chunk < chunks), chunk, chunk + chunks)
+    source = ((inner & (rows - 1)) >> 1) * message + block * CAP + (inner & 1)
+    gather = one_hot(iota((wide, window * message), 1) == source).astype(BF16)
+    for copy in z_copies:
+        copy.wait_recv()
+    gathered = contract(
+        gather, z_recv[...].reshape(window * message, LANES), 1, 0
+    ).astype(BF16)
+    for c in range(chunks + 1):
+        pack[q, :, c * LANES : (c + 1) * LANES] = gathered[c * 16 : (c + 1) * 16]
+
+    def all_plane(src, dst_of, send_sems, recv_sems):
+        copies = []
+        for d in range(1, plane):
+            target = q_up(d)
+            copies.append(
+                remote(src(target), dst_of(q), send_sems, recv_sems, d, in_plane(target))
+            )
+            copies[-1].start()
+        arrivals = [
+            remote(src(q_up(d)), dst_of(q_down(d)), send_sems, recv_sems, d, in_plane(q_up(d)))
+            for d in range(1, plane)
+        ]
+        return copies, arrivals
+
+    pk_copies, pk_arrivals = all_plane(lambda p: pack.at[q], lambda p: pack.at[p], pks, pkr)
+
+    for copy in w_copies:
+        copy.wait_recv()
+    router = w_recv[...].reshape(window * columns, depth)
+    for copy in pk_arrivals:
+        copy.wait_recv()
+
+    total = plane * rows
+    everything = pack[...].astype(F32)
+    x_rows = everything[:, :rows, :width].reshape(total, width).astype(BF16)
+    dy_rows = everything[:, rows:, :width].reshape(total, width).astype(BF16)
+    info = everything[:, :rows, width:].reshape(total, LANES)
+    xs[...] = x_rows
+    x_part = xs[:, pl.ds(pl.multiple_of(g * depth, LANES), depth)]
+
+    column = iota((total, window * columns), 1)
+    owner = lax.rem(z + window - column // columns, window)
+    column_id = ((owner * SPLIT + y) * columns + lax.rem(column, columns)).astype(F32)
+    hot = one_hot(info[:, 0:1] == column_id) - one_hot(info[:, 1:2] == column_id)
+    sign = info[:, 2:3]
+    gap_part = jnp.sum(contract(x_part, router, 1, 1) * hot, axis=1, keepdims=True)
+    row_diff = contract(hot.astype(BF16), router, 1, 0)
+    eye = iota((total, LANES), 0) == iota((total, LANES), 1)
+    gap_row = jnp.sum(jnp.where(eye, gap_part, 0.0), axis=0, keepdims=True)
+    gv_send[:, :, :depth] = row_diff.reshape(plane, rows, depth)
+    gv_send[:, :, depth:] = jnp.broadcast_to(gap_row[None], (plane, rows, LANES))
+    gv_recv[q] = gv_send[q]
+    gv_copies, gv_arrivals = all_plane(
+        lambda p: gv_send.at[p], lambda p: gv_recv.at[p], gvs, gvr
+    )
+
+    loads[3].wait()
+    back_up = contract(dy_rows, w2[...], 1, 1)
+    loads[2].wait()
+    pre_act = contract(x_rows, w1[...], 1, 0)
+    gelu_value, gelu_slope = gelu_parts(pre_act)
+    gate_part = jnp.sum(back_up * gelu_value, axis=1, keepdims=True)
+    gate_row = jnp.sum(jnp.where(eye, gate_part, 0.0), axis=0, keepdims=True)
+    gg[q] = jnp.broadcast_to(gate_row, (rows, LANES))
+    gg_copies, gg_arrivals = all_plane(lambda p: gg.at[q], lambda p: gg.at[p], ggs, ggr)
+
+    for copy in gv_arrivals:
+        copy.wait_recv()
+    gap_sum = jnp.sum(gv_recv[:, 0:1, depth:], axis=0)
+    gap = jnp.sum(jnp.where(eye, gap_sum, 0.0), axis=1, keepdims=True)
+    combine_first = jax.nn.sigmoid(gap)
+    combine_second = jax.nn.sigmoid(-gap)
+    gate = jnp.where(sign > 0.5, combine_first, jnp.where(sign < -0.5, combine_second, 0.0))
+    gate = gate.astype(BF16).astype(F32)
+    pre_grad = (gate * back_up * gelu_slope).astype(BF16)
+    part_rows = contract(pre_grad, w1[...], 1, 1).reshape(plane, rows, width)
+    half = width // 2
+    rp_send[...] = jnp.concatenate(
+        [part_rows[:, :, :half], part_rows[:, :, half:]], axis=1
+    ).astype(BF16)
+    rp_recv[q] = rp_send[q]
+    rp_copies, rp_arrivals = all_plane(
+        lambda p: rp_send.at[p], lambda p: rp_recv.at[p], rps, rpr
+    )
+
+    for copy in gg_arrivals:
+        copy.wait_recv()
+    grad_sum = jnp.sum(gg[:, 0:1, :], axis=0)
+    gate_grad = jnp.sum(jnp.where(eye, grad_sum, 0.0), axis=1, keepdims=True)
+    coef = sign * combine_first * combine_second * gate_grad
+    coef_ref[...] = jnp.broadcast_to(coef, (total, LANES))
+    logit_grad = coef * hot
+    high = logit_grad.astype(BF16)
+    low = (logit_grad - high.astype(F32)).astype(BF16)
+    router_part = contract(
+        jnp.concatenate([high, low], axis=0), jnp.concatenate([x_part, x_part], axis=0), 0, 0
+    )
+    for d in range(1, window):
+        rg_send[d] = router_part[d * columns : (d + 1) * columns].astype(BF16)
+    rg_copies = []
+    for d in range(1, window):
+        rg_copies.append(remote(rg_send.at[d], rg_recv.at[d], rgs, rgr, d, z_down(d)))
+        rg_copies[-1].start()
+
+    g1[...] = contract(x_rows, pre_grad, 0, 0).astype(BF16)
+    stores = [pltpu.make_async_copy(g1, w_in_grad_hbm.at[0], store_sems.at[0])]
+    stores[0].start()
+    scaled_grad = (gate * dy_rows.astype(F32)).astype(BF16)
+    g2[...] = contract(gelu_value.astype(BF16), scaled_grad, 0, 0).astype(BF16)
+    stores.append(pltpu.make_async_copy(g2, w_out_grad_hbm.at[0], store_sems.at[1]))
+    stores[1].start()
+
+    for copy in rp_arrivals:
+        copy.wait_recv()
+    summed = jnp.sum(rp_recv[...].astype(F32), axis=0)
+    row_grad = jnp.concatenate([summed[:rows], summed[rows:]], axis=1)
+    diffs = []
+    for part in range(groups):
+        diff = gv_recv[part, :, :depth]
+        for other in range(1, SPLIT):
+            diff = diff + gv_recv[other * groups + part, :, :depth]
+        diffs.append(diff)
+    own_coef = coef_ref[pl.ds(pl.multiple_of(q * rows, rows), rows), 0:1]
+    row_grad = row_grad + own_coef * jnp.concatenate(diffs, axis=1)
+    folded = jnp.concatenate(
+        [row_grad[:, c * LANES : (c + 1) * LANES] for c in range(chunks)], axis=0
+    ).astype(BF16)
+    back = chunks * rows
+    row = iota((back, back), 0)
+    source = ((row >> 1) & (chunks - 1)) * rows + (row >> 4) * CAP + (row & 1)
+    fold = one_hot(iota((back, back), 1) == source).astype(BF16)
+    ret_send[...] = contract(fold, folded, 1, 0).astype(BF16).reshape(ret_send.shape)
+    ret_recv[0] = ret_send[0]
+    ret_copies = []
+    for d in range(1, window):
+        ret_copies.append(remote(ret_send.at[d], ret_recv.at[d], rts, rtr, d, z_down(d)))
+        ret_copies[-1].start()
+
+    spread_back = jnp.transpose(place).astype(BF16)
+    for copy in rg_copies:
+        copy.wait_recv()
+    router_grad_ref[...] = router_part[:columns] + jnp.sum(
+        rg_recv[1:].astype(F32), axis=0
+    )
+
+    source = ((row >> 1) & (window - 1)) * 16 + (row >> 3) * CAP + (row & 1)
+    unfold = one_hot(iota((back, back), 1) == source).astype(BF16)
+    for copy in ret_copies:
+        copy.wait_recv()
+    flat = contract(unfold, ret_recv[...].reshape(back, LANES), 1, 0)
+    returned = jnp.concatenate(
+        [flat[c * rows : (c + 1) * rows] for c in range(chunks)], axis=1
+    )
+    returned = jnp.concatenate([returned, jnp.zeros((LANES - rows, width), F32)], axis=0)
+    in_grad_ref[...] = contract(spread_back, returned.astype(BF16), 1, 0).astype(BF16)
+
+    for group in (z_copies, w_copies, pk_copies, gv_copies, gg_copies, rp_copies, rg_copies, ret_copies):
+        for copy in group:
+            copy.wait_send()
+    for store in stores:
+        store.wait()
+
+
+def fused(tokens, out_grad, w_router, w_in, w_out, expert_ids, slot_ids, keep_mask):
+    window = lax.axis_size("expert") // SPLIT
+    groups = lax.axis_size("group")
+    plane = SPLIT * groups
+    count, width = tokens.shape
+    hidden = w_in.shape[2]
+    depth, columns = w_router.shape
+    rows = window * CAP
+    message = -(-CAP * (2 * width // LANES + 1) // 16) * 16
+    vmem = pl.BlockSpec(memory_space=pltpu.VMEM)
+    hbm = pl.BlockSpec(memory_space=pl.ANY)
+    dma = pltpu.SemaphoreType.DMA
+    in_grad, w_in_grad, w_out_grad, router_grad = pl.pallas_call(
+        functools.partial(fused_kernel, window, groups),
+        out_shape=(
+            jax.ShapeDtypeStruct((count, width), BF16),
+            jax.ShapeDtypeStruct(w_in.shape, BF16),
+            jax.ShapeDtypeStruct(w_out.shape, BF16),
+            jax.ShapeDtypeStruct((columns, depth), F32),
+        ),
+        in_specs=[hbm, hbm, vmem, hbm, hbm, vmem, vmem, vmem],
+        out_specs=(vmem, hbm, hbm, vmem),
+        scratch_shapes=[
+            pltpu.VMEM((count, width), BF16),
+            pltpu.VMEM((count, width), BF16),
+            pltpu.VMEM((width, hidden), BF16),
+            pltpu.VMEM((hidden, width), BF16),
+            pltpu.VMEM((width, hidden), BF16),
+            pltpu.VMEM((hidden, width), BF16),
+            pltpu.VMEM((window, message, LANES), BF16),
+            pltpu.VMEM((window, message, LANES), BF16),
+            pltpu.VMEM((window, columns, depth), BF16),
+            pltpu.VMEM((plane, 16, width + LANES), BF16),
+            pltpu.VMEM((plane * rows, width), BF16),
+            pltpu.VMEM((plane, rows, depth + LANES), F32),
+            pltpu.VMEM((plane, rows, depth + LANES), F32),
+            pltpu.VMEM((plane, rows, LANES), F32),
+            pltpu.VMEM((plane, 16, width // 2), BF16),
+            pltpu.VMEM((plane, 16, width // 2), BF16),
+            pltpu.VMEM((plane * rows, LANES), F32),
+            pltpu.VMEM((window, columns, depth), BF16),
+            pltpu.VMEM((window, columns, depth), BF16),
+            pltpu.VMEM((window, 16, LANES), BF16),
+            pltpu.VMEM((window, 16, LANES), BF16),
+            dma((4,)),
+            dma((2,)),
+        ]
+        + [dma((window,))] * 4
+        + [dma((plane,))] * 8
+        + [dma((window,))] * 4,
+        compiler_params=pltpu.CompilerParams(
+            collective_id=0, has_side_effects=True, vmem_limit_bytes=40 * 1024 * 1024
+        ),
+    )(
+        tokens,
+        out_grad,
+        w_router.T,
+        w_in,
+        w_out,
+        expert_ids.T,
+        slot_ids.T,
+        keep_mask.T,
+    )
+    return (in_grad, w_in_grad, w_out_grad, router_grad.T)
+
+
+def body(*args):
+    tokens, _, w_router = args[:3]
+    window = lax.axis_size("expert") // SPLIT
+    fits = (
+        window * CAP == 8
+        and w_router.shape[1] % 16 == 0
+        and w_router.shape[0] % LANES == 0
+        and window * w_router.shape[1] == LANES
+        and SPLIT * lax.axis_size("group") * window * CAP <= LANES
+        and tokens.shape == (LANES, 8 * LANES)
+    )
+    return fused(*args) if fits else gathered_body(*args)
+
+
 def solution(mesh):
     return jax.shard_map(
         body,

time: 228 us -> 36.7 us (0.16)
  waiting for transfers between devices: 104 us -> 0 us
  blocking collectives: 61.4 us -> 0 us
  starting transfers between devices: 27.7 us -> 0 us
  Pallas kernels: 0 us -> 26.7 us
  between operations: 15.2 us -> 0.67 us
  matrix products: 10.9 us -> 0 us
  local copies, waits for them, and re-layouts: 6.66 us -> 9.01 us
    reduce_scatter x3 -> x0, waiting for transfers between devices: 92.4 us -> none  [the longest x1 59.2 us: body(): lax.psum_scatter(router_sum, 'expert', scatter_dimension=1, tiled=True)]
    all_gather x4 -> x0, blocking collectives: 49.3 us -> none  [the longest x1 31.3 us: body(): lax.all_gather(w_router, 'expert', axis=1, tiled=True)]
    all_to_all x5 -> x0, starting transfers between devices: 27.6 us -> none  [the longest x1 7.28 us: body(): lax.all_to_all(token_send, 'expert', split_axis=0, concat_axis=0, tiled=T...]
    pallas_call x0 -> x1, Pallas kernels: none -> 26.7 us  [fused(): pl.pallas_call(functools.partial(fused_kernel, window, groups), out_shape...]
    unnamed x2 -> x0, blocking collectives: 12.1 us -> none
    all_to_all x5 -> x0, waiting for transfers between devices: 12 us -> none  [the longest x1 6.38 us: body(): lax.all_to_all(gate_sums.reshape(expert_count, CAP).astype(jnp.bfloat16),...]
    dot_general x11 -> x0, matrix products: 10.9 us -> none  [the longest x1 1.7 us: body(): jnp.dot(tokens.astype(jnp.float32).T, logit_grad, precision=lax.Precision...]
    unnamed x12 -> x20, local copies, waits for them, and re-layouts: 0.94 us -> 9.01 us
  transfers between devices with their start and end apart: 8 -> 0, of which waited for: 5 -> 0; matrix products, arithmetic and copies ran while one was open for 5% -> 0% of each run, Pallas kernels for 0% -> 0%
where the time goes in v1:
time: 36.7 us; the launch traced here: 36.4 us
  Pallas kernels  26.7 us (73%)
  local copies, waits for them, and re-layouts  9.01 us (25%)
  between operations  0.67 us (2%)
    pallas_call x1, Pallas kernels, fused(): pl.pallas_call(functools.partial(fused_kernel, window, groups), out_shape...  26.7 us
    unnamed x20, local copies, waits for them, and re-layouts  9.01 us

profile of v1, /device:TPU:0, one launch (start us, length us, event | category | flops | bytes accessed | tf_op | source)
XLA Modules:
  0.0 36.4 jit_solution(10535983703388036199)
XLA Ops:
  0.6 0.0 copy-start.6
  0.6 0.0 copy-start.7
  0.7 0.0 copy-start.5
  0.7 0.7 %copy-done.6 = s32[128,2]{0,1:T(2,128)S(1)} copy-done((s32[128,2]{0,1:T(2,128)S(1)}, s32[128,2]{0,1:T(2,128)}, u32[]{:S(2)}) %copy-start.6) | copy-done | bytes 1048
  1.3 0.0 copy-done.7
  1.3 0.0 copy-done.5
  1.3 0.0 copy-start
  1.3 1.2 %copy-done = bf16[1,1024,512]{2,1,0:T(8,128)(2,1)S(1)} copy-done((bf16[1,1024,512]{2,1,0:T(8,128)(2,1)S(1)}, bf16[1,1024,512]{2,1,0:T(8,128)(2,1)}, u32[]{:S(2)}) %copy-start) | copy-done | bytes 1048600
  2.6 0.0 copy-start.1
  2.6 1.2 %copy-done.1 = bf16[1,512,1024]{2,1,0:T(8,128)(2,1)S(1)} copy-done((bf16[1,512,1024]{2,1,0:T(8,128)(2,1)S(1)}, bf16[1,512,1024]{2,1,0:T(8,128)(2,1)}, u32[]{:S(2)}) %copy-start.1) | copy-done | bytes 1048600
  3.8 0.0 copy-start.2
  3.8 0.9 %copy-done.2 = bf16[128,1024]{1,0:T(8,128)(2,1)S(1)} copy-done((bf16[128,1024]{1,0:T(8,128)(2,1)S(1)}, bf16[128,1024]{1,0:T(8,128)(2,1)}, u32[]{:S(2)}) %copy-start.2) | copy-done | bytes 262168
  4.7 0.0 copy-start.3
  4.7 0.9 %copy-done.3 = bf16[128,1024]{1,0:T(8,128)(2,1)S(1)} copy-done((bf16[128,1024]{1,0:T(8,128)(2,1)S(1)}, bf16[128,1024]{1,0:T(8,128)(2,1)}, u32[]{:S(2)}) %copy-start.3) | copy-done | bytes 262168
  5.7 0.0 copy-start.4
  5.7 0.7 %copy-done.4 = bf16[256,32]{0,1:T(8,128)(2,1)S(1)} copy-done((bf16[256,32]{0,1:T(8,128)(2,1)S(1)}, bf16[256,32]{0,1:T(8,128)(2,1)}, u32[]{:S(2)}) %copy-start.4) | copy-done | bytes 16408
  6.4 26.7 %shard_map.111 = (bf16[128,1024]{1,0:T(8,128)(2,1)S(1)}, bf16[1,1024,512]{2,1,0:T(8,128)(2,1)S(1)}, bf16[1,512,1024]{2,1,0:T(8,128)(2,1)S(1)}, f32[32,256]{1,0:T(8,128)S(1)}) custom-call(bf16[128,1024]{1,0:T(8,128)(2,1)S(1)} %copy-done.2, bf16[128,1024]{1,0:T(8,128)(2,1)S(1)} %copy-done.3, bf16[32,256]{1,0:T(8,128)(2,1)S(1)} %bitcast.6, ...), custom_call_target="tpu_custom_call" | custom-call | tf_op jit(solution)/shard_map/pallas_call | solution.py:501
  33.1 0.7 %copy.16 = bf16[128,1024]{1,0:T(8,128)(2,1)} copy(bf16[128,1024]{1,0:T(8,128)(2,1)S(1)} %get-tuple-element.16) | data formatting | bytes 524288
  33.9 1.0 %copy.17 = bf16[1,1024,512]{2,1,0:T(8,128)(2,1)} copy(bf16[1,1024,512]{2,1,0:T(8,128)(2,1)S(1)} %get-tuple-element.17) | data formatting | bytes 2097152
  34.8 1.0 %copy.18 = bf16[1,512,1024]{2,1,0:T(8,128)(2,1)} copy(bf16[1,512,1024]{2,1,0:T(8,128)(2,1)S(1)} %get-tuple-element.18) | data formatting | bytes 2097152
  35.8 0.6 %copy.19 = f32[256,32]{0,1:T(8,128)} copy(f32[256,32]{0,1:T(8,128)S(1)} %bitcast.5) | data formatting | bytes 65536
Async XLA Ops:
  0.6 0.7 %copy-start.6 = (s32[128,2]{0,1:T(2,128)S(1)}, s32[128,2]{0,1:T(2,128)}, u32[]{:S(2)}) copy-start(s32[128,2]{0,1:T(2,128)} %param.14) | copy-start | bytes 3076
  0.6 0.7 %copy-start.7 = (s32[128,2]{0,1:T(2,128)S(1)}, s32[128,2]{0,1:T(2,128)}, u32[]{:S(2)}) copy-start(s32[128,2]{0,1:T(2,128)} %param.15) | copy-start | bytes 3076
  0.7 0.7 %copy-start.5 = (s32[128,2]{0,1:T(2,128)S(1)}, s32[128,2]{0,1:T(2,128)}, u32[]{:S(2)}) copy-start(s32[128,2]{0,1:T(2,128)} %param.13) | copy-start | bytes 3076
  1.3 1.2 %copy-start = (bf16[1,1024,512]{2,1,0:T(8,128)(2,1)S(1)}, bf16[1,1024,512]{2,1,0:T(8,128)(2,1)}, u32[]{:S(2)}) copy-start(bf16[1,1024,512]{2,1,0:T(8,128)(2,1)} %w_in_hbm.1) | copy-start | bytes 3145732
  2.6 1.2 %copy-start.1 = (bf16[1,512,1024]{2,1,0:T(8,128)(2,1)S(1)}, bf16[1,512,1024]{2,1,0:T(8,128)(2,1)}, u32[]{:S(2)}) copy-start(bf16[1,512,1024]{2,1,0:T(8,128)(2,1)} %w_out_hbm.1) | copy-start | bytes 3145732
  3.8 0.9 %copy-start.2 = (bf16[128,1024]{1,0:T(8,128)(2,1)S(1)}, bf16[128,1024]{1,0:T(8,128)(2,1)}, u32[]{:S(2)}) copy-start(bf16[128,1024]{1,0:T(8,128)(2,1)} %tokens_hbm.1) | copy-start | bytes 786436
  4.7 0.9 %copy-start.3 = (bf16[128,1024]{1,0:T(8,128)(2,1)S(1)}, bf16[128,1024]{1,0:T(8,128)(2,1)}, u32[]{:S(2)}) copy-start(bf16[128,1024]{1,0:T(8,128)(2,1)} %out_grad_hbm.1) | copy-start | bytes 786436
  5.7 0.7 %copy-start.4 = (bf16[256,32]{0,1:T(8,128)(2,1)S(1)}, bf16[256,32]{0,1:T(8,128)(2,1)}, u32[]{:S(2)}) copy-start(bf16[256,32]{0,1:T(8,128)(2,1)} %param.10) | copy-start | bytes 49156

commit v2 on v1

--- a/solution.py
+++ b/solution.py
@@ -157,21 +157,105 @@
     )
 
 
+def choice_places(z, window, ids_ref, slots_ref, keep_ref):
+    places = []
+    for k in range(2):
+        ids = ids_ref[k : k + 1, :]
+        relative = jnp.where(ids < z, ids - z + window, ids - z)
+        active = (keep_ref[k : k + 1, :] == 1) & (ids < window)
+        code = jnp.where(active, relative * CAP + slots_ref[k : k + 1, :], -1)
+        places.append(one_hot(iota((LANES, LANES), 0) == code))
+    return places
+
+
+def finish_kernel(
+    window,
+    g1_ref,
+    g2_ref,
+    returned_hbm,
+    router_ref,
+    ids_hbm,
+    slots_hbm,
+    keep_hbm,
+    in_grad_hbm,
+    w_in_grad_hbm,
+    w_out_grad_hbm,
+    router_grad_hbm,
+    in_grad,
+    returned_ref,
+    ids_ref,
+    slots_ref,
+    keep_ref,
+    sems,
+    load_sems,
+):
+    loads = [
+        pltpu.make_async_copy(src, dst, load_sems.at[i])
+        for i, (src, dst) in enumerate(
+            [
+                (ids_hbm, ids_ref),
+                (slots_hbm, slots_ref),
+                (keep_hbm, keep_ref),
+                (returned_hbm, returned_ref),
+            ]
+        )
+    ]
+    for load in loads:
+        load.start()
+    parts = 4
+    copies = []
+    for src, dst in ((g1_ref, w_in_grad_hbm.at[0]), (g2_ref, w_out_grad_hbm.at[0])):
+        step = src.shape[0] // parts
+        for p in range(parts):
+            span = pl.ds(p * step, step)
+            copies.append(pltpu.make_async_copy(src.at[span], dst.at[span], sems.at[len(copies)]))
+    copies.append(pltpu.make_async_copy(router_ref, router_grad_hbm, sems.at[2 * parts]))
+    for copy in copies:
+        copy.start()
+    for load in loads:
+        load.wait()
+    z = lax.axis_index("expert") // SPLIT
+    places = choice_places(z, window, ids_ref, slots_ref, keep_ref)
+    spread_back = jnp.transpose(places[0] + places[1]).astype(BF16)
+    rows = window * CAP
+    chunks = in_grad.shape[1] // LANES
+    back = chunks * rows
+    row = iota((back, back), 0)
+    source = ((row >> 1) & (window - 1)) * 16 + (row >> 3) * CAP + (row & 1)
+    unfold = one_hot(iota((back, back), 1) == source).astype(BF16)
+    flat = contract(unfold, returned_ref[...].reshape(back, LANES), 1, 0)
+    returned = jnp.concatenate(
+        [flat[c * rows : (c + 1) * rows] for c in range(chunks)], axis=1
+    )
+    returned = jnp.concatenate(
+        [returned, jnp.zeros((LANES - rows, chunks * LANES), F32)], axis=0
+    )
+    in_grad[...] = contract(spread_back, returned.astype(BF16), 1, 0).astype(BF16)
+    last = pltpu.make_async_copy(in_grad, in_grad_hbm, sems.at[2 * parts + 1])
+    last.start()
+    for copy in copies:
+        copy.wait()
+    last.wait()
+
+
 def fused_kernel(
     window,
     groups,
     tokens_hbm,
     out_grad_hbm,
-    router_ref,
+    router_hbm,
     w_in_hbm,
     w_out_hbm,
+    ids_hbm,
+    slots_hbm,
+    keep_hbm,
+    g1_out,
+    g2_out,
+    returned_ref,
+    router_grad_ref,
     ids_ref,
     slots_ref,
     keep_ref,
-    in_grad_ref,
-    w_in_grad_hbm,
-    w_out_grad_hbm,
-    router_grad_ref,
     tok,
     outg,
     w1,
@@ -218,7 +302,7 @@
     rows = window * CAP
     message = z_send.shape[1]
     used = CAP * (2 * chunks + 1)
-    columns, depth = router_ref.shape
+    columns, depth = router_hbm.shape
     ix = lax.axis_index("expert")
     g = lax.axis_index("group")
     z = ix // SPLIT
@@ -254,8 +338,12 @@
         pltpu.make_async_copy(src, dst, load_sems.at[i])
         for i, (src, dst) in enumerate(
             [
+                (ids_hbm, ids_ref),
+                (slots_hbm, slots_ref),
+                (keep_hbm, keep_ref),
                 (tokens_hbm, tok),
                 (out_grad_hbm, outg),
+                (router_hbm, w_recv.at[0]),
                 (w_in_hbm.at[0], w1),
                 (w_out_hbm.at[0], w2),
             ]
@@ -270,13 +358,9 @@
     for d in range(1, plane):
         pl.semaphore_signal(barrier, inc=1, device_id=in_plane(q_up(d)), device_id_type=MESH)
 
-    places = []
-    for k in range(2):
-        ids = ids_ref[k : k + 1, :]
-        relative = jnp.where(ids < z, ids - z + window, ids - z)
-        active = (keep_ref[k : k + 1, :] == 1) & (ids < window)
-        code = jnp.where(active, relative * CAP + slots_ref[k : k + 1, :], -1)
-        places.append(one_hot(iota((LANES, LANES), 0) == code))
+    for load in loads[:3]:
+        load.wait()
+    places = choice_places(z, window, ids_ref, slots_ref, keep_ref)
     place = places[0] + places[1]
     place_rows = place[:16].astype(BF16)
     short = place[:rows]
@@ -288,8 +372,8 @@
         lane == 0, first_id, jnp.where(lane == 1, second_id, jnp.where(lane == 2, which, 0.0))
     )
 
-    loads[0].wait()
-    loads[1].wait()
+    loads[3].wait()
+    loads[4].wait()
     x_slots = contract(place_rows, tok[...], 1, 0)[:rows]
     dy_slots = contract(place_rows, outg[...], 1, 0)[:rows]
     pieces = [x_slots[:, c * LANES : (c + 1) * LANES] for c in range(chunks)]
@@ -306,16 +390,15 @@
     z_recv[0] = messages[:message]
     for d in range(1, window):
         z_send[d] = messages[d * message : (d + 1) * message]
-    w_recv[0] = router_ref[...]
-
     pl.semaphore_wait(barrier, window - 1 + plane - 1)
 
     z_copies, w_copies = [], []
     for d in range(1, window):
         z_copies.append(remote(z_send.at[d], z_recv.at[d], zs, zr, d, z_up(d)))
         z_copies[-1].start()
+    loads[5].wait()
     for d in range(1, window):
-        w_copies.append(remote(router_ref, w_recv.at[d], ws, wr, d, z_up(d)))
+        w_copies.append(remote(w_recv.at[0], w_recv.at[d], ws, wr, d, z_up(d)))
         w_copies[-1].start()
 
     wide = (chunks + 1) * 16
@@ -379,9 +462,9 @@
         lambda p: gv_send.at[p], lambda p: gv_recv.at[p], gvs, gvr
     )
 
-    loads[3].wait()
+    loads[7].wait()
     back_up = contract(dy_rows, w2[...], 1, 1)
-    loads[2].wait()
+    loads[6].wait()
     pre_act = contract(x_rows, w1[...], 1, 0)
     gelu_value, gelu_slope = gelu_parts(pre_act)
     gate_part = jnp.sum(back_up * gelu_value, axis=1, keepdims=True)
@@ -428,11 +511,11 @@
         rg_copies[-1].start()
 
     g1[...] = contract(x_rows, pre_grad, 0, 0).astype(BF16)
-    stores = [pltpu.make_async_copy(g1, w_in_grad_hbm.at[0], store_sems.at[0])]
+    stores = [pltpu.make_async_copy(g1, g1_out, store_sems.at[0])]
     stores[0].start()
     scaled_grad = (gate * dy_rows.astype(F32)).astype(BF16)
     g2[...] = contract(gelu_value.astype(BF16), scaled_grad, 0, 0).astype(BF16)
-    stores.append(pltpu.make_async_copy(g2, w_out_grad_hbm.at[0], store_sems.at[1]))
+    stores.append(pltpu.make_async_copy(g2, g2_out, store_sems.at[1]))
     stores[1].start()
 
     for copy in rp_arrivals:
@@ -461,23 +544,15 @@
         ret_copies.append(remote(ret_send.at[d], ret_recv.at[d], rts, rtr, d, z_down(d)))
         ret_copies[-1].start()
 
-    spread_back = jnp.transpose(place).astype(BF16)
     for copy in rg_copies:
         copy.wait_recv()
     router_grad_ref[...] = router_part[:columns] + jnp.sum(
         rg_recv[1:].astype(F32), axis=0
     )
 
-    source = ((row >> 1) & (window - 1)) * 16 + (row >> 3) * CAP + (row & 1)
-    unfold = one_hot(iota((back, back), 1) == source).astype(BF16)
     for copy in ret_copies:
         copy.wait_recv()
-    flat = contract(unfold, ret_recv[...].reshape(back, LANES), 1, 0)
-    returned = jnp.concatenate(
-        [flat[c * rows : (c + 1) * rows] for c in range(chunks)], axis=1
-    )
-    returned = jnp.concatenate([returned, jnp.zeros((LANES - rows, width), F32)], axis=0)
-    in_grad_ref[...] = contract(spread_back, returned.astype(BF16), 1, 0).astype(BF16)
+    returned_ref[...] = ret_recv[...]
 
     for group in (z_copies, w_copies, pk_copies, gv_copies, gg_copies, rp_copies, rg_copies, ret_copies):
         for copy in group:
@@ -496,19 +571,24 @@
     rows = window * CAP
     message = -(-CAP * (2 * width // LANES + 1) // 16) * 16
     vmem = pl.BlockSpec(memory_space=pltpu.VMEM)
-    hbm = pl.BlockSpec(memory_space=pl.ANY)
+    free = pl.BlockSpec(memory_space=pl.ANY)
+    hbm = pl.BlockSpec(memory_space=pltpu.HBM)
     dma = pltpu.SemaphoreType.DMA
-    in_grad, w_in_grad, w_out_grad, router_grad = pl.pallas_call(
+    routing = (expert_ids.T, slot_ids.T, keep_mask.T)
+    g1, g2, returned, router_part = pl.pallas_call(
         functools.partial(fused_kernel, window, groups),
         out_shape=(
-            jax.ShapeDtypeStruct((count, width), BF16),
-            jax.ShapeDtypeStruct(w_in.shape, BF16),
-            jax.ShapeDtypeStruct(w_out.shape, BF16),
+            jax.ShapeDtypeStruct((width, hidden), BF16),
+            jax.ShapeDtypeStruct((hidden, width), BF16),
+            jax.ShapeDtypeStruct((window, 16, LANES), BF16),
             jax.ShapeDtypeStruct((columns, depth), F32),
         ),
-        in_specs=[hbm, hbm, vmem, hbm, hbm, vmem, vmem, vmem],
-        out_specs=(vmem, hbm, hbm, vmem),
+        in_specs=[hbm] * 8,
+        out_specs=(free, free, vmem, vmem),
         scratch_shapes=[
+            pltpu.VMEM(expert_ids.shape[::-1], jnp.int32),
+            pltpu.VMEM(slot_ids.shape[::-1], jnp.int32),
+            pltpu.VMEM(keep_mask.shape[::-1], jnp.int32),
             pltpu.VMEM((count, width), BF16),
             pltpu.VMEM((count, width), BF16),
             pltpu.VMEM((width, hidden), BF16),
@@ -530,14 +610,14 @@
             pltpu.VMEM((window, columns, depth), BF16),
             pltpu.VMEM((window, 16, LANES), BF16),
             pltpu.VMEM((window, 16, LANES), BF16),
-            dma((4,)),
+            dma((8,)),
             dma((2,)),
         ]
         + [dma((window,))] * 4
         + [dma((plane,))] * 8
         + [dma((window,))] * 4,
         compiler_params=pltpu.CompilerParams(
-            collective_id=0, has_side_effects=True, vmem_limit_bytes=40 * 1024 * 1024
+            collective_id=0, has_side_effects=True, vmem_limit_bytes=60 * 1024 * 1024
         ),
     )(
         tokens,
@@ -545,10 +625,29 @@
         w_router.T,
         w_in,
         w_out,
-        expert_ids.T,
-        slot_ids.T,
-        keep_mask.T,
-    )
+        *routing,
+    )
+    in_grad, w_in_grad, w_out_grad, router_grad = pl.pallas_call(
+        functools.partial(finish_kernel, window),
+        out_shape=(
+            jax.ShapeDtypeStruct((count, width), BF16),
+            jax.ShapeDtypeStruct(w_in.shape, BF16),
+            jax.ShapeDtypeStruct(w_out.shape, BF16),
+            jax.ShapeDtypeStruct((columns, depth), F32),
+        ),
+        in_specs=[hbm] * 7,
+        out_specs=(hbm, hbm, hbm, hbm),
+        scratch_shapes=[
+            pltpu.VMEM((count, width), BF16),
+            pltpu.VMEM((window, 16, LANES), BF16),
+            pltpu.VMEM(expert_ids.shape[::-1], jnp.int32),
+            pltpu.VMEM(slot_ids.shape[::-1], jnp.int32),
+            pltpu.VMEM(keep_mask.shape[::-1], jnp.int32),
+            dma((10,)),
+            dma((4,)),
+        ],
+        compiler_params=pltpu.CompilerParams(vmem_limit_bytes=60 * 1024 * 1024),
+    )(g1, g2, returned, router_part, *routing)
     return (in_grad, w_in_grad, w_out_grad, router_grad.T)
 
 

time: 36.7 us -> 93.5 us (2.55)
  Pallas kernels: 26.7 us -> 92.7 us
  local copies, waits for them, and re-layouts: 9.01 us -> 0 us
    pallas_call x0 -> x1, Pallas kernels: none -> 65.8 us  [fused(): pl.pallas_call(functools.partial(finish_kernel, window), out_shape=(jax.S...]
    unnamed x20 -> x0, local copies, waits for them, and re-layouts: 9.01 us -> none
where the time goes in v2:
time: 93.5 us; the launch traced here: 93.3 us
  Pallas kernels  92.7 us (99%)
    pallas_call x1, Pallas kernels, fused(): pl.pallas_call(functools.partial(finish_kernel, window), out_shape=(jax.S...  65.8 us
    pallas_call x1, Pallas kernels, fused(): pl.pallas_call(functools.partial(fused_kernel, window, groups), out_shape...  26.9 us

profile of v2, /device:TPU:0, one launch (start us, length us, event | category | flops | bytes accessed | tf_op | source)
XLA Modules:
  0.0 93.3 jit_solution(4394303343608147731)
XLA Ops:
  0.6 26.9 %shard_map.111 = (bf16[1024,512]{1,0:T(8,128)(2,1)}, bf16[512,1024]{1,0:T(8,128)(2,1)}, bf16[4,16,128]{2,1,0:T(8,128)(2,1)}, f32[32,256]{1,0:T(8,128)}) custom-call(bf16[128,1024]{1,0:T(8,128)(2,1)} %tokens_hbm.1, bf16[128,1024]{1,0:T(8,128)(2,1)} %out_grad_hbm.1, bf16[32,256]{1,0:T(8,128)(2,1)} %bitcast.5, bf16[1,1024,512]{2,1,0:T(8,128)(2,1)} %w_in_hbm.1, ...), custom_call_target="tpu_custom_call" | custom-call | tf_op jit(solution)/shard_map/pallas_call | solution.py:578
  27.5 65.8 %shard_map.112 = (bf16[128,1024]{1,0:T(8,128)(2,1)}, bf16[1,1024,512]{2,1,0:T(8,128)(2,1)}, bf16[1,512,1024]{2,1,0:T(8,128)(2,1)}, f32[32,256]{1,0:T(8,128)}) custom-call(bf16[1024,512]{1,0:T(8,128)(2,1)} %get-tuple-element.12.g1_ref, bf16[512,1024]{1,0:T(8,128)(2,1)} %get-tuple-element.13.g2_ref, bf16[4,16,128]{2,1,0:T(8,128)(2,1)} %get-tuple-element.14.returned_hbm, ...), custom_call_target="tpu_custom_call" | custom-call | tf_op jit(solution)/shard_map/pallas_call | solution.py:630

commit v3 on v2

--- a/solution.py
+++ b/solution.py
@@ -170,8 +170,10 @@
 
 def finish_kernel(
     window,
-    g1_ref,
-    g2_ref,
+    x_hbm,
+    pre_grad_hbm,
+    hidden_hbm,
+    scaled_hbm,
     returned_hbm,
     router_ref,
     ids_hbm,
@@ -181,6 +183,13 @@
     w_in_grad_hbm,
     w_out_grad_hbm,
     router_grad_hbm,
+    x_rows,
+    pre_grad,
+    hidden,
+    scaled,
+    router_grad,
+    g1,
+    g2,
     in_grad,
     returned_ref,
     ids_ref,
@@ -193,10 +202,15 @@
         pltpu.make_async_copy(src, dst, load_sems.at[i])
         for i, (src, dst) in enumerate(
             [
+                (x_hbm, x_rows),
+                (pre_grad_hbm, pre_grad),
+                (hidden_hbm, hidden),
+                (scaled_hbm, scaled),
+                (returned_hbm, returned_ref),
+                (router_ref, router_grad),
                 (ids_hbm, ids_ref),
                 (slots_hbm, slots_ref),
                 (keep_hbm, keep_ref),
-                (returned_hbm, returned_ref),
             ]
         )
     ]
@@ -204,16 +218,27 @@
         load.start()
     parts = 4
     copies = []
-    for src, dst in ((g1_ref, w_in_grad_hbm.at[0]), (g2_ref, w_out_grad_hbm.at[0])):
-        step = src.shape[0] // parts
+
+    def weight_grad(left, right, staged, target):
+        step = staged.shape[0] // parts
         for p in range(parts):
             span = pl.ds(p * step, step)
-            copies.append(pltpu.make_async_copy(src.at[span], dst.at[span], sems.at[len(copies)]))
-    copies.append(pltpu.make_async_copy(router_ref, router_grad_hbm, sems.at[2 * parts]))
-    for copy in copies:
-        copy.start()
-    for load in loads:
+            staged[span] = contract(left[:, span], right[...], 0, 0).astype(BF16)
+            copies.append(
+                pltpu.make_async_copy(staged.at[span], target.at[span], sems.at[len(copies)])
+            )
+            copies[-1].start()
+
+    loads[0].wait()
+    loads[1].wait()
+    weight_grad(x_rows, pre_grad, g1, w_in_grad_hbm.at[0])
+    loads[2].wait()
+    loads[3].wait()
+    weight_grad(hidden, scaled, g2, w_out_grad_hbm.at[0])
+    for load in loads[4:]:
         load.wait()
+    copies.append(pltpu.make_async_copy(router_grad, router_grad_hbm, sems.at[2 * parts]))
+    copies[-1].start()
     z = lax.axis_index("expert") // SPLIT
     places = choice_places(z, window, ids_ref, slots_ref, keep_ref)
     spread_back = jnp.transpose(places[0] + places[1]).astype(BF16)
@@ -231,11 +256,10 @@
         [returned, jnp.zeros((LANES - rows, chunks * LANES), F32)], axis=0
     )
     in_grad[...] = contract(spread_back, returned.astype(BF16), 1, 0).astype(BF16)
-    last = pltpu.make_async_copy(in_grad, in_grad_hbm, sems.at[2 * parts + 1])
-    last.start()
+    copies.append(pltpu.make_async_copy(in_grad, in_grad_hbm, sems.at[2 * parts + 1]))
+    copies[-1].start()
     for copy in copies:
         copy.wait()
-    last.wait()
 
 
 def fused_kernel(
@@ -249,8 +273,10 @@
     ids_hbm,
     slots_hbm,
     keep_hbm,
-    g1_out,
-    g2_out,
+    x_out,
+    pre_grad_out,
+    hidden_out,
+    scaled_out,
     returned_ref,
     router_grad_ref,
     ids_ref,
@@ -260,12 +286,14 @@
     outg,
     w1,
     w2,
-    g1,
-    g2,
+    pre_grad_ref,
+    hidden_ref,
+    scaled_ref,
     z_send,
     z_recv,
     w_recv,
-    pack,
+    x_pack,
+    dy_pack,
     xs,
     gv_send,
     gv_recv,
@@ -283,8 +311,10 @@
     zr,
     ws,
     wr,
-    pks,
-    pkr,
+    xps,
+    xpr,
+    dps,
+    dpr,
     gvs,
     gvr,
     ggs,
@@ -401,11 +431,18 @@
         w_copies.append(remote(w_recv.at[0], w_recv.at[d], ws, wr, d, z_up(d)))
         w_copies[-1].start()
 
+    half = width // 2
+    side = chunks // 2
     wide = (chunks + 1) * 16
     row = iota((wide, window * message), 0)
     inner = row & 15
-    chunk = row >> 4
-    block = jnp.where((inner < rows) & (chunk < chunks), chunk, chunk + chunks)
+    column = row >> 4
+    upper = jnp.where(inner < rows, 0, side)
+    block = jnp.where(
+        column < side,
+        column + upper,
+        jnp.where(column == side, 2 * chunks, chunks + column - side - 1 + upper),
+    )
     source = ((inner & (rows - 1)) >> 1) * message + block * CAP + (inner & 1)
     gather = one_hot(iota((wide, window * message), 1) == source).astype(BF16)
     for copy in z_copies:
@@ -413,36 +450,52 @@
     gathered = contract(
         gather, z_recv[...].reshape(window * message, LANES), 1, 0
     ).astype(BF16)
-    for c in range(chunks + 1):
-        pack[q, :, c * LANES : (c + 1) * LANES] = gathered[c * 16 : (c + 1) * 16]
-
-    def all_plane(src, dst_of, send_sems, recv_sems):
+    for c in range(side + 1):
+        x_pack[q, :, c * LANES : (c + 1) * LANES] = gathered[c * 16 : (c + 1) * 16]
+    for c in range(side):
+        first = (side + 1 + c) * 16
+        dy_pack[q, :, c * LANES : (c + 1) * LANES] = gathered[first : first + 16]
+
+    def all_plane(src, dst_of, send_sems, recv_sems, base=0):
         copies = []
         for d in range(1, plane):
             target = q_up(d)
             copies.append(
-                remote(src(target), dst_of(q), send_sems, recv_sems, d, in_plane(target))
+                remote(
+                    src(target), dst_of(q), send_sems, recv_sems, base + d, in_plane(target)
+                )
             )
             copies[-1].start()
         arrivals = [
-            remote(src(q_up(d)), dst_of(q_down(d)), send_sems, recv_sems, d, in_plane(q_up(d)))
+            remote(
+                src(q_up(d)), dst_of(q_down(d)), send_sems, recv_sems, base + d, in_plane(q_up(d))
+            )
             for d in range(1, plane)
         ]
         return copies, arrivals
 
-    pk_copies, pk_arrivals = all_plane(lambda p: pack.at[q], lambda p: pack.at[p], pks, pkr)
+    def unfolded(block):
+        return jnp.concatenate(
+            [block[:, :rows, :half], block[:, rows:, :half]], axis=2
+        ).reshape(plane * rows, width)
+
+    xp_copies, xp_arrivals = all_plane(
+        lambda p: x_pack.at[q], lambda p: x_pack.at[p], xps, xpr
+    )
+    dp_copies, dp_arrivals = all_plane(
+        lambda p: dy_pack.at[q], lambda p: dy_pack.at[p], dps, dpr
+    )
 
     for copy in w_copies:
         copy.wait_recv()
     router = w_recv[...].reshape(window * columns, depth)
-    for copy in pk_arrivals:
+    for copy in xp_arrivals:
         copy.wait_recv()
 
     total = plane * rows
-    everything = pack[...].astype(F32)
-    x_rows = everything[:, :rows, :width].reshape(total, width).astype(BF16)
-    dy_rows = everything[:, rows:, :width].reshape(total, width).astype(BF16)
-    info = everything[:, :rows, width:].reshape(total, LANES)
+    packed = x_pack[...].astype(F32)
+    x_rows = unfolded(packed).astype(BF16)
+    info = packed[:, :rows, half:].reshape(total, LANES)
     xs[...] = x_rows
     x_part = xs[:, pl.ds(pl.multiple_of(g * depth, LANES), depth)]
 
@@ -462,10 +515,13 @@
         lambda p: gv_send.at[p], lambda p: gv_recv.at[p], gvs, gvr
     )
 
-    loads[7].wait()
-    back_up = contract(dy_rows, w2[...], 1, 1)
     loads[6].wait()
     pre_act = contract(x_rows, w1[...], 1, 0)
+    loads[7].wait()
+    for copy in dp_arrivals:
+        copy.wait_recv()
+    dy_rows = unfolded(dy_pack[...].astype(F32)).astype(BF16)
+    back_up = contract(dy_rows, w2[...], 1, 1)
     gelu_value, gelu_slope = gelu_parts(pre_act)
     gate_part = jnp.sum(back_up * gelu_value, axis=1, keepdims=True)
     gate_row = jnp.sum(jnp.where(eye, gate_part, 0.0), axis=0, keepdims=True)
@@ -481,15 +537,23 @@
     gate = jnp.where(sign > 0.5, combine_first, jnp.where(sign < -0.5, combine_second, 0.0))
     gate = gate.astype(BF16).astype(F32)
     pre_grad = (gate * back_up * gelu_slope).astype(BF16)
-    part_rows = contract(pre_grad, w1[...], 1, 1).reshape(plane, rows, width)
-    half = width // 2
-    rp_send[...] = jnp.concatenate(
-        [part_rows[:, :, :half], part_rows[:, :, half:]], axis=1
-    ).astype(BF16)
-    rp_recv[q] = rp_send[q]
-    rp_copies, rp_arrivals = all_plane(
-        lambda p: rp_send.at[p], lambda p: rp_recv.at[p], rps, rpr
-    )
+    rp_copies, rp_arrivals = [], []
+    for h in range(2):
+        part = contract(pre_grad, w1[h * half : (h + 1) * half, :], 1, 1)
+        part = part.reshape(plane, rows, half)
+        rp_send[h] = jnp.concatenate(
+            [part[:, :, : half // 2], part[:, :, half // 2 :]], axis=1
+        ).astype(BF16)
+        rp_recv[h, q] = rp_send[h, q]
+        started, arriving = all_plane(
+            lambda p, h=h: rp_send.at[h, p],
+            lambda p, h=h: rp_recv.at[h, p],
+            rps,
+            rpr,
+            h * plane,
+        )
+        rp_copies += started
+        rp_arrivals.append(arriving)
 
     for copy in gg_arrivals:
         copy.wait_recv()
@@ -510,18 +574,30 @@
         rg_copies.append(remote(rg_send.at[d], rg_recv.at[d], rgs, rgr, d, z_down(d)))
         rg_copies[-1].start()
 
-    g1[...] = contract(x_rows, pre_grad, 0, 0).astype(BF16)
-    stores = [pltpu.make_async_copy(g1, g1_out, store_sems.at[0])]
-    stores[0].start()
-    scaled_grad = (gate * dy_rows.astype(F32)).astype(BF16)
-    g2[...] = contract(gelu_value.astype(BF16), scaled_grad, 0, 0).astype(BF16)
-    stores.append(pltpu.make_async_copy(g2, g2_out, store_sems.at[1]))
-    stores[1].start()
-
-    for copy in rp_arrivals:
-        copy.wait_recv()
-    summed = jnp.sum(rp_recv[...].astype(F32), axis=0)
-    row_grad = jnp.concatenate([summed[:rows], summed[rows:]], axis=1)
+    pre_grad_ref[...] = pre_grad
+    hidden_ref[...] = gelu_value.astype(BF16)
+    scaled_ref[...] = (gate * dy_rows.astype(F32)).astype(BF16)
+    stores = [
+        pltpu.make_async_copy(src, dst, store_sems.at[i])
+        for i, (src, dst) in enumerate(
+            [
+                (xs, x_out),
+                (pre_grad_ref, pre_grad_out),
+                (hidden_ref, hidden_out),
+                (scaled_ref, scaled_out),
+            ]
+        )
+    ]
+    for store in stores:
+        store.start()
+
+    halves = []
+    for h in range(2):
+        for copy in rp_arrivals[h]:
+            copy.wait_recv()
+        summed = jnp.sum(rp_recv[h].astype(F32), axis=0)
+        halves += [summed[:rows], summed[rows:]]
+    row_grad = jnp.concatenate(halves, axis=1)
     diffs = []
     for part in range(groups):
         diff = gv_recv[part, :, :depth]
@@ -554,7 +630,17 @@
         copy.wait_recv()
     returned_ref[...] = ret_recv[...]
 
-    for group in (z_copies, w_copies, pk_copies, gv_copies, gg_copies, rp_copies, rg_copies, ret_copies):
+    for group in (
+        z_copies,
+        w_copies,
+        xp_copies,
+        dp_copies,
+        gv_copies,
+        gg_copies,
+        rp_copies,
+        rg_copies,
+        ret_copies,
+    ):
         for copy in group:
             copy.wait_send()
     for store in stores:
@@ -571,20 +657,22 @@
     rows = window * CAP
     message = -(-CAP * (2 * width // LANES + 1) // 16) * 16
     vmem = pl.BlockSpec(memory_space=pltpu.VMEM)
-    free = pl.BlockSpec(memory_space=pl.ANY)
     hbm = pl.BlockSpec(memory_space=pltpu.HBM)
     dma = pltpu.SemaphoreType.DMA
     routing = (expert_ids.T, slot_ids.T, keep_mask.T)
-    g1, g2, returned, router_part = pl.pallas_call(
+    total = plane * rows
+    *handed, returned, router_part = pl.pallas_call(
         functools.partial(fused_kernel, window, groups),
         out_shape=(
-            jax.ShapeDtypeStruct((width, hidden), BF16),
-            jax.ShapeDtypeStruct((hidden, width), BF16),
+            jax.ShapeDtypeStruct((total, width), BF16),
+            jax.ShapeDtypeStruct((total, hidden), BF16),
+            jax.ShapeDtypeStruct((total, hidden), BF16),
+            jax.ShapeDtypeStruct((total, width), BF16),
             jax.ShapeDtypeStruct((window, 16, LANES), BF16),
             jax.ShapeDtypeStruct((columns, depth), F32),
         ),
         in_specs=[hbm] * 8,
-        out_specs=(free, free, vmem, vmem),
+        out_specs=(hbm, hbm, hbm, hbm, vmem, vmem),
         scratch_shapes=[
             pltpu.VMEM(expert_ids.shape[::-1], jnp.int32),
             pltpu.VMEM(slot_ids.shape[::-1], jnp.int32),
@@ -593,28 +681,31 @@
             pltpu.VMEM((count, width), BF16),
             pltpu.VMEM((width, hidden), BF16),
             pltpu.VMEM((hidden, width), BF16),
-            pltpu.VMEM((width, hidden), BF16),
-            pltpu.VMEM((hidden, width), BF16),
+            pltpu.VMEM((total, hidden), BF16),
+            pltpu.VMEM((total, hidden), BF16),
+            pltpu.VMEM((total, width), BF16),
             pltpu.VMEM((window, message, LANES), BF16),
             pltpu.VMEM((window, message, LANES), BF16),
             pltpu.VMEM((window, columns, depth), BF16),
-            pltpu.VMEM((plane, 16, width + LANES), BF16),
+            pltpu.VMEM((plane, 16, width // 2 + LANES), BF16),
+            pltpu.VMEM((plane, 16, width // 2), BF16),
             pltpu.VMEM((plane * rows, width), BF16),
             pltpu.VMEM((plane, rows, depth + LANES), F32),
             pltpu.VMEM((plane, rows, depth + LANES), F32),
             pltpu.VMEM((plane, rows, LANES), F32),
-            pltpu.VMEM((plane, 16, width // 2), BF16),
-            pltpu.VMEM((plane, 16, width // 2), BF16),
+            pltpu.VMEM((2, plane, 16, width // 4), BF16),
+            pltpu.VMEM((2, plane, 16, width // 4), BF16),
             pltpu.VMEM((plane * rows, LANES), F32),
             pltpu.VMEM((window, columns, depth), BF16),
             pltpu.VMEM((window, columns, depth), BF16),
             pltpu.VMEM((window, 16, LANES), BF16),
             pltpu.VMEM((window, 16, LANES), BF16),
             dma((8,)),
-            dma((2,)),
+            dma((4,)),
         ]
         + [dma((window,))] * 4
         + [dma((plane,))] * 8
+        + [dma((2 * plane,))] * 2
         + [dma((window,))] * 4,
         compiler_params=pltpu.CompilerParams(
             collective_id=0, has_side_effects=True, vmem_limit_bytes=60 * 1024 * 1024
@@ -635,19 +726,26 @@
             jax.ShapeDtypeStruct(w_out.shape, BF16),
             jax.ShapeDtypeStruct((columns, depth), F32),
         ),
-        in_specs=[hbm] * 7,
+        in_specs=[hbm] * 9,
         out_specs=(hbm, hbm, hbm, hbm),
         scratch_shapes=[
+            pltpu.VMEM((total, width), BF16),
+            pltpu.VMEM((total, hidden), BF16),
+            pltpu.VMEM((total, hidden), BF16),
+            pltpu.VMEM((total, width), BF16),
+            pltpu.VMEM((columns, depth), F32),
+            pltpu.VMEM((width, hidden), BF16),
+            pltpu.VMEM((hidden, width), BF16),
             pltpu.VMEM((count, width), BF16),
             pltpu.VMEM((window, 16, LANES), BF16),
             pltpu.VMEM(expert_ids.shape[::-1], jnp.int32),
             pltpu.VMEM(slot_ids.shape[::-1], jnp.int32),
             pltpu.VMEM(keep_mask.shape[::-1], jnp.int32),
             dma((10,)),
-            dma((4,)),
+            dma((9,)),
         ],
         compiler_params=pltpu.CompilerParams(vmem_limit_bytes=60 * 1024 * 1024),
-    )(g1, g2, returned, router_part, *routing)
+    )(*handed, returned, router_part, *routing)
     return (in_grad, w_in_grad, w_out_grad, router_grad.T)
 
 

time: 93.5 us -> 30.6 us (0.33)
  Pallas kernels: 92.7 us -> 29.8 us
    pallas_call x1, Pallas kernels: 65.8 us -> 3.03 us  [fused(): pl.pallas_call(functools.partial(finish_kernel, window), out_shape=(jax.S...]
where the time goes in v3:
time: 30.6 us; the launch traced here: 30.4 us
  Pallas kernels  29.8 us (97%)
  between operations  0.64 us (2%)
    pallas_call x1, Pallas kernels, fused(): pl.pallas_call(functools.partial(fused_kernel, window, groups), out_shape...  26.8 us
    pallas_call x1, Pallas kernels, fused(): pl.pallas_call(functools.partial(finish_kernel, window), out_shape=(jax.S...  3.03 us

profile of v3, /device:TPU:0, one launch (start us, length us, event | category | flops | bytes accessed | tf_op | source)
XLA Modules:
  0.0 30.4 jit_solution(11592678515121265114)
XLA Ops:
  0.6 26.8 %shard_map.111 = (bf16[64,1024]{1,0:T(8,128)(2,1)}, bf16[64,512]{1,0:T(8,128)(2,1)}, bf16[64,512]{1,0:T(8,128)(2,1)}, bf16[64,1024]{1,0:T(8,128)(2,1)}, bf16[4,16,128]{2,1,0:T(8,128)(2,1)}, /*index=5*/f32[32,256]{1,0:T(8,128)}) custom-call(bf16[128,1024]{1,0:T(8,128)(2,1)} %tokens_hbm.1, bf16[128,1024]{1,0:T(8,128)(2,1)} %out_grad_hbm.1, ...), custom_call_target="tpu_custom_call" | custom-call | tf_op jit(solution)/shard_map/pallas_call | solution.py:664
  27.4 3.0 %shard_map.112 = (bf16[128,1024]{1,0:T(8,128)(2,1)}, bf16[1,1024,512]{2,1,0:T(8,128)(2,1)}, bf16[1,512,1024]{2,1,0:T(8,128)(2,1)}, f32[32,256]{1,0:T(8,128)}) custom-call(bf16[64,1024]{1,0:T(8,128)(2,1)} %get-tuple-element.14.x_hbm, bf16[64,512]{1,0:T(8,128)(2,1)} %get-tuple-element.15.pre_grad_hbm, bf16[64,512]{1,0:T(8,128)(2,1)} %get-tuple-element.16.hidden_hbm, ...), custom_call_target="tpu_custom_call" | custom-call | tf_op jit(solution)/shard_map/pallas_call | solution.py:721

commit v4 on v3

--- a/solution.py
+++ b/solution.py
@@ -308,23 +308,14 @@
     load_sems,
     store_sems,
     zs,
-    zr,
     ws,
-    wr,
     xps,
-    xpr,
     dps,
-    dpr,
     gvs,
-    gvr,
     ggs,
-    ggr,
     rps,
-    rpr,
     rgs,
-    rgr,
     rts,
-    rtr,
 ):
     plane = SPLIT * groups
     width = tok.shape[1]
@@ -354,15 +345,34 @@
     def q_down(d):
         return lax.rem(q + plane - d, plane)
 
-    def remote(src, dst, send_sems, recv_sems, d, target):
+    def remote(src, dst, sems, target):
         return pltpu.make_async_remote_copy(
             src_ref=src,
             dst_ref=dst,
-            send_sem=send_sems.at[d],
-            recv_sem=recv_sems.at[d],
+            send_sem=sems.at[0],
+            recv_sem=sems.at[1],
             device_id=target,
             device_id_type=MESH,
         )
+
+    def along_z(src, dst, sems, target_of):
+        for d in range(1, window):
+            remote(src(d), dst.at[d], sems, target_of(d)).start()
+        every = dst.at[pl.ds(1, window - 1)]
+        return remote(every, every, sems, target_of(1))
+
+    def all_plane(src, dst, sems):
+        for d in range(1, plane):
+            target = q_up(d)
+            remote(src(target), dst.at[q], sems, in_plane(target)).start()
+        every = dst.at[pl.ds(0, plane - 1)]
+        return remote(every, every, sems, in_plane(q_up(1)))
+
+    barrier = pltpu.get_barrier_semaphore()
+    for d in range(1, window):
+        pl.semaphore_signal(barrier, inc=1, device_id=z_up(d), device_id_type=MESH)
+    for d in range(1, plane):
+        pl.semaphore_signal(barrier, inc=1, device_id=in_plane(q_up(d)), device_id_type=MESH)
 
     loads = [
         pltpu.make_async_copy(src, dst, load_sems.at[i])
@@ -382,11 +392,27 @@
     for load in loads:
         load.start()
 
-    barrier = pltpu.get_barrier_semaphore()
-    for d in range(1, window):
-        pl.semaphore_signal(barrier, inc=1, device_id=z_up(d), device_id_type=MESH)
-    for d in range(1, plane):
-        pl.semaphore_signal(barrier, inc=1, device_id=in_plane(q_up(d)), device_id_type=MESH)
+    depth_f = (2 * chunks + 2) * rows
+    spread = []
+    for d in range(window):
+        row = iota((message, depth_f), 0)
+        source = (row >> 1) * rows + d * CAP + (row & 1)
+        spread.append(one_hot((iota((message, depth_f), 1) == source) & (row < used)))
+    spread = jnp.concatenate(spread, axis=0).astype(BF16)
+    half = width // 2
+    side = chunks // 2
+    wide = (chunks + 1) * 16
+    row = iota((wide, window * message), 0)
+    inner = row & 15
+    column = row >> 4
+    upper = jnp.where(inner < rows, 0, side)
+    block = jnp.where(
+        column < side,
+        column + upper,
+        jnp.where(column == side, 2 * chunks, chunks + column - side - 1 + upper),
+    )
+    source = ((inner & (rows - 1)) >> 1) * message + block * CAP + (inner & 1)
+    gather = one_hot(iota((wide, window * message), 1) == source).astype(BF16)
 
     for load in loads[:3]:
         load.wait()
@@ -410,43 +436,16 @@
     pieces += [dy_slots[:, c * LANES : (c + 1) * LANES] for c in range(chunks)]
     pieces += [meta, jnp.zeros((rows, LANES), F32)]
     folded = jnp.concatenate(pieces, axis=0).astype(BF16)
-    depth_f = folded.shape[0]
-    spread = []
-    for d in range(window):
-        row = iota((message, depth_f), 0)
-        source = (row >> 1) * rows + d * CAP + (row & 1)
-        spread.append(one_hot((iota((message, depth_f), 1) == source) & (row < used)))
-    messages = contract(jnp.concatenate(spread, axis=0).astype(BF16), folded, 1, 0).astype(BF16)
+    messages = contract(spread, folded, 1, 0).astype(BF16)
     z_recv[0] = messages[:message]
     for d in range(1, window):
         z_send[d] = messages[d * message : (d + 1) * message]
     pl.semaphore_wait(barrier, window - 1 + plane - 1)
 
-    z_copies, w_copies = [], []
-    for d in range(1, window):
-        z_copies.append(remote(z_send.at[d], z_recv.at[d], zs, zr, d, z_up(d)))
-        z_copies[-1].start()
+    z_all = along_z(lambda d: z_send.at[d], z_recv, zs, z_up)
     loads[5].wait()
-    for d in range(1, window):
-        w_copies.append(remote(w_recv.at[0], w_recv.at[d], ws, wr, d, z_up(d)))
-        w_copies[-1].start()
-
-    half = width // 2
-    side = chunks // 2
-    wide = (chunks + 1) * 16
-    row = iota((wide, window * message), 0)
-    inner = row & 15
-    column = row >> 4
-    upper = jnp.where(inner < rows, 0, side)
-    block = jnp.where(
-        column < side,
-        column + upper,
-        jnp.where(column == side, 2 * chunks, chunks + column - side - 1 + upper),
-    )
-    source = ((inner & (rows - 1)) >> 1) * message + block * CAP + (inner & 1)
-    gather = one_hot(iota((wide, window * message), 1) == source).astype(BF16)
-    for copy in z_copies:
-        copy.wait_recv()
+    w_all = along_z(lambda d: w_recv.at[0], w_recv, ws, z_up)
+    z_all.wait_recv()
     gathered = contract(
         gather, z_recv[...].reshape(window * message, LANES), 1, 0
     ).astype(BF16)
@@ -456,41 +455,17 @@
         first = (side + 1 + c) * 16
         dy_pack[q, :, c * LANES : (c + 1) * LANES] = gathered[first : first + 16]
 
-    def all_plane(src, dst_of, send_sems, recv_sems, base=0):
-        copies = []
-        for d in range(1, plane):
-            target = q_up(d)
-            copies.append(
-                remote(
-                    src(target), dst_of(q), send_sems, recv_sems, base + d, in_plane(target)
-                )
-            )
-            copies[-1].start()
-        arrivals = [
-            remote(
-                src(q_up(d)), dst_of(q_down(d)), send_sems, recv_sems, base + d, in_plane(q_up(d))
-            )
-            for d in range(1, plane)
-        ]
-        return copies, arrivals
-
     def unfolded(block):
         return jnp.concatenate(
             [block[:, :rows, :half], block[:, rows:, :half]], axis=2
         ).reshape(plane * rows, width)
 
-    xp_copies, xp_arrivals = all_plane(
-        lambda p: x_pack.at[q], lambda p: x_pack.at[p], xps, xpr
-    )
-    dp_copies, dp_arrivals = all_plane(
-        lambda p: dy_pack.at[q], lambda p: dy_pack.at[p], dps, dpr
-    )
-
-    for copy in w_copies:
-        copy.wait_recv()
+    xp_all = all_plane(lambda p: x_pack.at[q], x_pack, xps)
+    dp_all = all_plane(lambda p: dy_pack.at[q], dy_pack, dps)
+    z_all.wait_send()
+    w_all.wait()
     router = w_recv[...].reshape(window * columns, depth)
-    for copy in xp_arrivals:
-        copy.wait_recv()
+    xp_all.wait_recv()
 
     total = plane * rows
     packed = x_pack[...].astype(F32)
@@ -511,25 +486,21 @@
     gv_send[:, :, :depth] = row_diff.reshape(plane, rows, depth)
     gv_send[:, :, depth:] = jnp.broadcast_to(gap_row[None], (plane, rows, LANES))
     gv_recv[q] = gv_send[q]
-    gv_copies, gv_arrivals = all_plane(
-        lambda p: gv_send.at[p], lambda p: gv_recv.at[p], gvs, gvr
-    )
+    gv_all = all_plane(lambda p: gv_send.at[p], gv_recv, gvs)
 
     loads[6].wait()
     pre_act = contract(x_rows, w1[...], 1, 0)
     loads[7].wait()
-    for copy in dp_arrivals:
-        copy.wait_recv()
+    dp_all.wait_recv()
     dy_rows = unfolded(dy_pack[...].astype(F32)).astype(BF16)
     back_up = contract(dy_rows, w2[...], 1, 1)
     gelu_value, gelu_slope = gelu_parts(pre_act)
     gate_part = jnp.sum(back_up * gelu_value, axis=1, keepdims=True)
     gate_row = jnp.sum(jnp.where(eye, gate_part, 0.0), axis=0, keepdims=True)
     gg[q] = jnp.broadcast_to(gate_row, (rows, LANES))
-    gg_copies, gg_arrivals = all_plane(lambda p: gg.at[q], lambda p: gg.at[p], ggs, ggr)
-
-    for copy in gv_arrivals:
-        copy.wait_recv()
+    gg_all = all_plane(lambda p: gg.at[q], gg, ggs)
+
+    gv_all.wait_recv()
     gap_sum = jnp.sum(gv_recv[:, 0:1, depth:], axis=0)
     gap = jnp.sum(jnp.where(eye, gap_sum, 0.0), axis=1, keepdims=True)
     combine_first = jax.nn.sigmoid(gap)
@@ -537,7 +508,7 @@
     gate = jnp.where(sign > 0.5, combine_first, jnp.where(sign < -0.5, combine_second, 0.0))
     gate = gate.astype(BF16).astype(F32)
     pre_grad = (gate * back_up * gelu_slope).astype(BF16)
-    rp_copies, rp_arrivals = [], []
+    rp_all = []
     for h in range(2):
         part = contract(pre_grad, w1[h * half : (h + 1) * half, :], 1, 1)
         part = part.reshape(plane, rows, half)
@@ -545,18 +516,9 @@
             [part[:, :, : half // 2], part[:, :, half // 2 :]], axis=1
         ).astype(BF16)
         rp_recv[h, q] = rp_send[h, q]
-        started, arriving = all_plane(
-            lambda p, h=h: rp_send.at[h, p],
-            lambda p, h=h: rp_recv.at[h, p],
-            rps,
-            rpr,
-            h * plane,
-        )
-        rp_copies += started
-        rp_arrivals.append(arriving)
-
-    for copy in gg_arrivals:
-        copy.wait_recv()
+        rp_all.append(all_plane(lambda p, h=h: rp_send.at[h, p], rp_recv.at[h], rps.at[h]))
+
+    gg_all.wait_recv()
     grad_sum = jnp.sum(gg[:, 0:1, :], axis=0)
     gate_grad = jnp.sum(jnp.where(eye, grad_sum, 0.0), axis=1, keepdims=True)
     coef = sign * combine_first * combine_second * gate_grad
@@ -569,10 +531,7 @@
     )
     for d in range(1, window):
         rg_send[d] = router_part[d * columns : (d + 1) * columns].astype(BF16)
-    rg_copies = []
-    for d in range(1, window):
-        rg_copies.append(remote(rg_send.at[d], rg_recv.at[d], rgs, rgr, d, z_down(d)))
-        rg_copies[-1].start()
+    rg_all = along_z(lambda d: rg_send.at[d], rg_recv, rgs, z_down)
 
     pre_grad_ref[...] = pre_grad
     hidden_ref[...] = gelu_value.astype(BF16)
@@ -591,10 +550,11 @@
     for store in stores:
         store.start()
 
+    for sent in (xp_all, dp_all, gv_all, gg_all):
+        sent.wait_send()
     halves = []
     for h in range(2):
-        for copy in rp_arrivals[h]:
-            copy.wait_recv()
+        rp_all[h].wait_recv()
         summed = jnp.sum(rp_recv[h].astype(F32), axis=0)
         halves += [summed[:rows], summed[rows:]]
     row_grad = jnp.concatenate(halves, axis=1)
@@ -615,36 +575,18 @@
     fold = one_hot(iota((back, back), 1) == source).astype(BF16)
     ret_send[...] = contract(fold, folded, 1, 0).astype(BF16).reshape(ret_send.shape)
     ret_recv[0] = ret_send[0]
-    ret_copies = []
-    for d in range(1, window):
-        ret_copies.append(remote(ret_send.at[d], ret_recv.at[d], rts, rtr, d, z_down(d)))
-        ret_copies[-1].start()
-
-    for copy in rg_copies:
-        copy.wait_recv()
+    ret_all = along_z(lambda d: ret_send.at[d], ret_recv, rts, z_down)
+
+    for sent in (*rp_all, rg_all):
+        sent.wait_send()
+    for store in stores:
+        store.wait()
+    rg_all.wait_recv()
     router_grad_ref[...] = router_part[:columns] + jnp.sum(
         rg_recv[1:].astype(F32), axis=0
     )
-
-    for copy in ret_copies:
-        copy.wait_recv()
+    ret_all.wait()
     returned_ref[...] = ret_recv[...]
-
-    for group in (
-        z_copies,
-        w_copies,
-        xp_copies,
-        dp_copies,
-        gv_copies,
-        gg_copies,
-        rp_copies,
-        rg_copies,
-        ret_copies,
-    ):
-        for copy in group:
-            copy.wait_send()
-    for store in stores:
-        store.wait()
 
 
 def fused(tokens, out_grad, w_router, w_in, w_out, expert_ids, slot_ids, keep_mask):
@@ -703,10 +645,9 @@
             dma((8,)),
             dma((4,)),
         ]
-        + [dma((window,))] * 4
-        + [dma((plane,))] * 8
-        + [dma((2 * plane,))] * 2
-        + [dma((window,))] * 4,
+        + [dma((2,))] * 6
+        + [dma((2, 2))]
+        + [dma((2,))] * 2,
         compiler_params=pltpu.CompilerParams(
             collective_id=0, has_side_effects=True, vmem_limit_bytes=60 * 1024 * 1024
         ),

time: 30.6 us -> 29.5 us (0.964)
  Pallas kernels: 29.8 us -> 28.7 us
    pallas_call x1, Pallas kernels: 26.8 us -> 25.7 us  [fused(): pl.pallas_call(functools.partial(fused_kernel, window, groups), out_shape...]
where the time goes in v4:
time: 29.5 us; the launch traced here: 29.4 us
  Pallas kernels  28.7 us (97%)
  between operations  0.64 us (2%)
    pallas_call x1, Pallas kernels, fused(): pl.pallas_call(functools.partial(fused_kernel, window, groups), out_shape...  25.7 us
    pallas_call x1, Pallas kernels, fused(): pl.pallas_call(functools.partial(finish_kernel, window), out_shape=(jax.S...  3.03 us

profile of v4, /device:TPU:0, one launch (start us, length us, event | category | flops | bytes accessed | tf_op | source)
XLA Modules:
  0.0 29.4 jit_solution(16927172611040863803)
XLA Ops:
  0.6 25.7 %shard_map.111 = (bf16[64,1024]{1,0:T(8,128)(2,1)}, bf16[64,512]{1,0:T(8,128)(2,1)}, bf16[64,512]{1,0:T(8,128)(2,1)}, bf16[64,1024]{1,0:T(8,128)(2,1)}, bf16[4,16,128]{2,1,0:T(8,128)(2,1)}, /*index=5*/f32[32,256]{1,0:T(8,128)}) custom-call(bf16[128,1024]{1,0:T(8,128)(2,1)} %tokens_hbm.1, bf16[128,1024]{1,0:T(8,128)(2,1)} %out_grad_hbm.1, ...), custom_call_target="tpu_custom_call" | custom-call | tf_op jit(solution)/shard_map/pallas_call | solution.py:606
  26.3 3.0 %shard_map.112 = (bf16[128,1024]{1,0:T(8,128)(2,1)}, bf16[1,1024,512]{2,1,0:T(8,128)(2,1)}, bf16[1,512,1024]{2,1,0:T(8,128)(2,1)}, f32[32,256]{1,0:T(8,128)}) custom-call(bf16[64,1024]{1,0:T(8,128)(2,1)} %get-tuple-element.14.x_hbm, bf16[64,512]{1,0:T(8,128)(2,1)} %get-tuple-element.15.pre_grad_hbm, bf16[64,512]{1,0:T(8,128)(2,1)} %get-tuple-element.16.hidden_hbm, ...), custom_call_target="tpu_custom_call" | custom-call | tf_op jit(solution)/shard_map/pallas_call | solution.py:662

commit v5 on v4

--- a/solution.py
+++ b/solution.py
@@ -157,25 +157,23 @@
     )
 
 
-def choice_places(z, window, ids_ref, slots_ref, keep_ref):
+def choice_places(count, z, window, ids_ref, slots_ref, keep_ref):
     places = []
     for k in range(2):
         ids = ids_ref[k : k + 1, :]
         relative = jnp.where(ids < z, ids - z + window, ids - z)
         active = (keep_ref[k : k + 1, :] == 1) & (ids < window)
         code = jnp.where(active, relative * CAP + slots_ref[k : k + 1, :], -1)
-        places.append(one_hot(iota((LANES, LANES), 0) == code))
+        places.append(one_hot(iota((count, LANES), 0) == code))
     return places
 
 
 def finish_kernel(
     window,
-    x_hbm,
-    pre_grad_hbm,
-    hidden_hbm,
-    scaled_hbm,
+    g1_hbm,
+    g2_hbm,
     returned_hbm,
-    router_ref,
+    router_hbm,
     ids_hbm,
     slots_hbm,
     keep_hbm,
@@ -183,13 +181,9 @@
     w_in_grad_hbm,
     w_out_grad_hbm,
     router_grad_hbm,
-    x_rows,
-    pre_grad,
-    hidden,
-    scaled,
-    router_grad,
     g1,
     g2,
+    router_grad,
     in_grad,
     returned_ref,
     ids_ref,
@@ -198,68 +192,65 @@
     sems,
     load_sems,
 ):
-    loads = [
-        pltpu.make_async_copy(src, dst, load_sems.at[i])
-        for i, (src, dst) in enumerate(
-            [
-                (x_hbm, x_rows),
-                (pre_grad_hbm, pre_grad),
-                (hidden_hbm, hidden),
-                (scaled_hbm, scaled),
-                (returned_hbm, returned_ref),
-                (router_ref, router_grad),
-                (ids_hbm, ids_ref),
-                (slots_hbm, slots_ref),
-                (keep_hbm, keep_ref),
-            ]
-        )
-    ]
+    parts = 4
+    loads, stores = [], []
+    for src, staged, dst, pieces in (
+        (ids_hbm, ids_ref, None, 1),
+        (slots_hbm, slots_ref, None, 1),
+        (keep_hbm, keep_ref, None, 1),
+        (returned_hbm, returned_ref, None, 1),
+        (router_hbm, router_grad, router_grad_hbm, 1),
+        (g1_hbm, g1, w_in_grad_hbm.at[0], parts),
+        (g2_hbm, g2, w_out_grad_hbm.at[0], parts),
+    ):
+        step = src.shape[0] // pieces
+        for p in range(pieces):
+            span = pl.ds(p * step, step)
+            whole = pieces == 1
+            loads.append(
+                pltpu.make_async_copy(
+                    src if whole else src.at[span],
+                    staged if whole else staged.at[span],
+                    load_sems.at[len(loads)],
+                )
+            )
+            if dst is not None:
+                stores.append(
+                    pltpu.make_async_copy(
+                        staged if whole else staged.at[span],
+                        dst if whole else dst.at[span],
+                        sems.at[len(stores)],
+                    )
+                )
     for load in loads:
         load.start()
-    parts = 4
-    copies = []
-
-    def weight_grad(left, right, staged, target):
-        step = staged.shape[0] // parts
-        for p in range(parts):
-            span = pl.ds(p * step, step)
-            staged[span] = contract(left[:, span], right[...], 0, 0).astype(BF16)
-            copies.append(
-                pltpu.make_async_copy(staged.at[span], target.at[span], sems.at[len(copies)])
-            )
-            copies[-1].start()
-
-    loads[0].wait()
-    loads[1].wait()
-    weight_grad(x_rows, pre_grad, g1, w_in_grad_hbm.at[0])
-    loads[2].wait()
-    loads[3].wait()
-    weight_grad(hidden, scaled, g2, w_out_grad_hbm.at[0])
-    for load in loads[4:]:
-        load.wait()
-    copies.append(pltpu.make_async_copy(router_grad, router_grad_hbm, sems.at[2 * parts]))
-    copies[-1].start()
-    z = lax.axis_index("expert") // SPLIT
-    places = choice_places(z, window, ids_ref, slots_ref, keep_ref)
-    spread_back = jnp.transpose(places[0] + places[1]).astype(BF16)
     rows = window * CAP
     chunks = in_grad.shape[1] // LANES
     back = chunks * rows
     row = iota((back, back), 0)
     source = ((row >> 1) & (window - 1)) * 16 + (row >> 3) * CAP + (row & 1)
     unfold = one_hot(iota((back, back), 1) == source).astype(BF16)
+    z = lax.axis_index("expert") // SPLIT
+    for load in loads[:3]:
+        load.wait()
+    places = choice_places(LANES, z, window, ids_ref, slots_ref, keep_ref)
+    spread_back = jnp.transpose(places[0] + places[1]).astype(BF16)
+    loads[3].wait()
     flat = contract(unfold, returned_ref[...].reshape(back, LANES), 1, 0)
     returned = jnp.concatenate(
         [flat[c * rows : (c + 1) * rows] for c in range(chunks)], axis=1
     )
     returned = jnp.concatenate(
         [returned, jnp.zeros((LANES - rows, chunks * LANES), F32)], axis=0
-    )
-    in_grad[...] = contract(spread_back, returned.astype(BF16), 1, 0).astype(BF16)
-    copies.append(pltpu.make_async_copy(in_grad, in_grad_hbm, sems.at[2 * parts + 1]))
-    copies[-1].start()
-    for copy in copies:
-        copy.wait()
+    ).astype(BF16)
+    for load, store in zip(loads[4:], stores):
+        load.wait()
+        store.start()
+    in_grad[...] = contract(spread_back, returned, 1, 0).astype(BF16)
+    stores.append(pltpu.make_async_copy(in_grad, in_grad_hbm, sems.at[len(stores)]))
+    stores[-1].start()
+    for store in stores:
+        store.wait()
 
 
 def fused_kernel(
@@ -273,12 +264,10 @@
     ids_hbm,
     slots_hbm,
     keep_hbm,
-    x_out,
-    pre_grad_out,
-    hidden_out,
-    scaled_out,
-    returned_ref,
-    router_grad_ref,
+    g1_out,
+    g2_out,
+    returned_out,
+    router_grad_out,
     ids_ref,
     slots_ref,
     keep_ref,
@@ -286,9 +275,9 @@
     outg,
     w1,
     w2,
-    pre_grad_ref,
-    hidden_ref,
-    scaled_ref,
+    g1,
+    g2,
+    router_grad_ref,
     z_send,
     z_recv,
     w_recv,
@@ -416,9 +405,9 @@
 
     for load in loads[:3]:
         load.wait()
-    places = choice_places(z, window, ids_ref, slots_ref, keep_ref)
+    places = choice_places(16, z, window, ids_ref, slots_ref, keep_ref)
     place = places[0] + places[1]
-    place_rows = place[:16].astype(BF16)
+    place_rows = place.astype(BF16)
     short = place[:rows]
     first_id = jnp.sum(short * ids_ref[0:1, :].astype(F32), axis=1, keepdims=True)
     second_id = jnp.sum(short * ids_ref[1:2, :].astype(F32), axis=1, keepdims=True)
@@ -443,6 +432,11 @@
     pl.semaphore_wait(barrier, window - 1 + plane - 1)
 
     z_all = along_z(lambda d: z_send.at[d], z_recv, zs, z_up)
+    total = plane * rows
+    eye = iota((total, LANES), 0) == iota((total, LANES), 1)
+    column = iota((1, window * columns), 1)
+    owner = lax.rem(z + window - column // columns, window)
+    column_id = ((owner * SPLIT + y) * columns + lax.rem(column, columns)).astype(F32)
     loads[5].wait()
     w_all = along_z(lambda d: w_recv.at[0], w_recv, ws, z_up)
     z_all.wait_recv()
@@ -467,21 +461,16 @@
     router = w_recv[...].reshape(window * columns, depth)
     xp_all.wait_recv()
 
-    total = plane * rows
     packed = x_pack[...].astype(F32)
     x_rows = unfolded(packed).astype(BF16)
     info = packed[:, :rows, half:].reshape(total, LANES)
     xs[...] = x_rows
     x_part = xs[:, pl.ds(pl.multiple_of(g * depth, LANES), depth)]
 
-    column = iota((total, window * columns), 1)
-    owner = lax.rem(z + window - column // columns, window)
-    column_id = ((owner * SPLIT + y) * columns + lax.rem(column, columns)).astype(F32)
     hot = one_hot(info[:, 0:1] == column_id) - one_hot(info[:, 1:2] == column_id)
     sign = info[:, 2:3]
     gap_part = jnp.sum(contract(x_part, router, 1, 1) * hot, axis=1, keepdims=True)
     row_diff = contract(hot.astype(BF16), router, 1, 0)
-    eye = iota((total, LANES), 0) == iota((total, LANES), 1)
     gap_row = jnp.sum(jnp.where(eye, gap_part, 0.0), axis=0, keepdims=True)
     gv_send[:, :, :depth] = row_diff.reshape(plane, rows, depth)
     gv_send[:, :, depth:] = jnp.broadcast_to(gap_row[None], (plane, rows, LANES))
@@ -533,23 +522,35 @@
         rg_send[d] = router_part[d * columns : (d + 1) * columns].astype(BF16)
     rg_all = along_z(lambda d: rg_send.at[d], rg_recv, rgs, z_down)
 
-    pre_grad_ref[...] = pre_grad
-    hidden_ref[...] = gelu_value.astype(BF16)
-    scaled_ref[...] = (gate * dy_rows.astype(F32)).astype(BF16)
-    stores = [
-        pltpu.make_async_copy(src, dst, store_sems.at[i])
-        for i, (src, dst) in enumerate(
-            [
-                (xs, x_out),
-                (pre_grad_ref, pre_grad_out),
-                (hidden_ref, hidden_out),
-                (scaled_ref, scaled_out),
-            ]
-        )
-    ]
-    for store in stores:
-        store.start()
-
+    diffs = []
+    for part in range(groups):
+        diff = gv_recv[part, :, :depth]
+        for other in range(1, SPLIT):
+            diff = diff + gv_recv[other * groups + part, :, :depth]
+        diffs.append(diff)
+    own_coef = coef_ref[pl.ds(pl.multiple_of(q * rows, rows), rows), 0:1]
+    router_rows = own_coef * jnp.concatenate(diffs, axis=1)
+    back = chunks * rows
+    row = iota((back, back), 0)
+    source = ((row >> 1) & (chunks - 1)) * rows + (row >> 4) * CAP + (row & 1)
+    fold = one_hot(iota((back, back), 1) == source).astype(BF16)
+
+    stores = []
+
+    def weight_grad(left, right, staged, target):
+        parts = 4
+        step = staged.shape[0] // parts
+        for p in range(parts):
+            span = slice(p * step, (p + 1) * step)
+            staged[span] = contract(left[:, span], right, 0, 0).astype(BF16)
+            stores.append(
+                pltpu.make_async_copy(
+                    staged.at[span], target.at[span], store_sems.at[len(stores)]
+                )
+            )
+            stores[-1].start()
+
+    weight_grad(x_rows, pre_grad, g1, g1_out)
     for sent in (xp_all, dp_all, gv_all, gg_all):
         sent.wait_send()
     halves = []
@@ -558,35 +559,34 @@
         summed = jnp.sum(rp_recv[h].astype(F32), axis=0)
         halves += [summed[:rows], summed[rows:]]
     row_grad = jnp.concatenate(halves, axis=1)
-    diffs = []
-    for part in range(groups):
-        diff = gv_recv[part, :, :depth]
-        for other in range(1, SPLIT):
-            diff = diff + gv_recv[other * groups + part, :, :depth]
-        diffs.append(diff)
-    own_coef = coef_ref[pl.ds(pl.multiple_of(q * rows, rows), rows), 0:1]
-    row_grad = row_grad + own_coef * jnp.concatenate(diffs, axis=1)
+    row_grad = row_grad + router_rows
     folded = jnp.concatenate(
         [row_grad[:, c * LANES : (c + 1) * LANES] for c in range(chunks)], axis=0
     ).astype(BF16)
-    back = chunks * rows
-    row = iota((back, back), 0)
-    source = ((row >> 1) & (chunks - 1)) * rows + (row >> 4) * CAP + (row & 1)
-    fold = one_hot(iota((back, back), 1) == source).astype(BF16)
     ret_send[...] = contract(fold, folded, 1, 0).astype(BF16).reshape(ret_send.shape)
     ret_recv[0] = ret_send[0]
     ret_all = along_z(lambda d: ret_send.at[d], ret_recv, rts, z_down)
 
-    for sent in (*rp_all, rg_all):
-        sent.wait_send()
-    for store in stores:
-        store.wait()
     rg_all.wait_recv()
     router_grad_ref[...] = router_part[:columns] + jnp.sum(
         rg_recv[1:].astype(F32), axis=0
     )
-    ret_all.wait()
-    returned_ref[...] = ret_recv[...]
+    stores.append(
+        pltpu.make_async_copy(router_grad_ref, router_grad_out, store_sems.at[len(stores)])
+    )
+    stores[-1].start()
+    scaled_grad = (gate * dy_rows.astype(F32)).astype(BF16)
+    weight_grad(gelu_value.astype(BF16), scaled_grad, g2, g2_out)
+    for sent in (*rp_all, rg_all):
+        sent.wait_send()
+    ret_all.wait_recv()
+    stores.append(
+        pltpu.make_async_copy(ret_recv, returned_out, store_sems.at[len(stores)])
+    )
+    stores[-1].start()
+    ret_all.wait_send()
+    for store in stores:
+        store.wait()
 
 
 def fused(tokens, out_grad, w_router, w_in, w_out, expert_ids, slot_ids, keep_mask):
@@ -598,23 +598,19 @@
     depth, columns = w_router.shape
     rows = window * CAP
     message = -(-CAP * (2 * width // LANES + 1) // 16) * 16
-    vmem = pl.BlockSpec(memory_space=pltpu.VMEM)
     hbm = pl.BlockSpec(memory_space=pltpu.HBM)
     dma = pltpu.SemaphoreType.DMA
     routing = (expert_ids.T, slot_ids.T, keep_mask.T)
-    total = plane * rows
-    *handed, returned, router_part = pl.pallas_call(
+    g1, g2, returned, router_part = pl.pallas_call(
         functools.partial(fused_kernel, window, groups),
         out_shape=(
-            jax.ShapeDtypeStruct((total, width), BF16),
-            jax.ShapeDtypeStruct((total, hidden), BF16),
-            jax.ShapeDtypeStruct((total, hidden), BF16),
-            jax.ShapeDtypeStruct((total, width), BF16),
+            jax.ShapeDtypeStruct((width, hidden), BF16),
+            jax.ShapeDtypeStruct((hidden, width), BF16),
             jax.ShapeDtypeStruct((window, 16, LANES), BF16),
             jax.ShapeDtypeStruct((columns, depth), F32),
         ),
         in_specs=[hbm] * 8,
-        out_specs=(hbm, hbm, hbm, hbm, vmem, vmem),
+        out_specs=(hbm, hbm, hbm, hbm),
         scratch_shapes=[
             pltpu.VMEM(expert_ids.shape[::-1], jnp.int32),
             pltpu.VMEM(slot_ids.shape[::-1], jnp.int32),
@@ -623,9 +619,9 @@
             pltpu.VMEM((count, width), BF16),
             pltpu.VMEM((width, hidden), BF16),
             pltpu.VMEM((hidden, width), BF16),
-            pltpu.VMEM((total, hidden), BF16),
-            pltpu.VMEM((total, hidden), BF16),
-            pltpu.VMEM((total, width), BF16),
+            pltpu.VMEM((width, hidden), BF16),
+            pltpu.VMEM((hidden, width), BF16),
+            pltpu.VMEM((columns, depth), F32),
             pltpu.VMEM((window, message, LANES), BF16),
             pltpu.VMEM((window, message, LANES), BF16),
             pltpu.VMEM((window, columns, depth), BF16),
@@ -643,7 +639,7 @@
             pltpu.VMEM((window, 16, LANES), BF16),
             pltpu.VMEM((window, 16, LANES), BF16),
             dma((8,)),
-            dma((4,)),
+            dma((10,)),
         ]
         + [dma((2,))] * 6
         + [dma((2, 2))]
@@ -667,26 +663,22 @@
             jax.ShapeDtypeStruct(w_out.shape, BF16),
             jax.ShapeDtypeStruct((columns, depth), F32),
         ),
-        in_specs=[hbm] * 9,
+        in_specs=[hbm] * 7,
         out_specs=(hbm, hbm, hbm, hbm),
         scratch_shapes=[
-            pltpu.VMEM((total, width), BF16),
-            pltpu.VMEM((total, hidden), BF16),
-            pltpu.VMEM((total, hidden), BF16),
-            pltpu.VMEM((total, width), BF16),
-            pltpu.VMEM((columns, depth), F32),
             pltpu.VMEM((width, hidden), BF16),
             pltpu.VMEM((hidden, width), BF16),
+            pltpu.VMEM((columns, depth), F32),
             pltpu.VMEM((count, width), BF16),
             pltpu.VMEM((window, 16, LANES), BF16),
             pltpu.VMEM(expert_ids.shape[::-1], jnp.int32),
             pltpu.VMEM(slot_ids.shape[::-1], jnp.int32),
             pltpu.VMEM(keep_mask.shape[::-1], jnp.int32),
             dma((10,)),
-            dma((9,)),
+            dma((13,)),
         ],
         compiler_params=pltpu.CompilerParams(vmem_limit_bytes=60 * 1024 * 1024),
-    )(*handed, returned, router_part, *routing)
+    )(g1, g2, returned, router_part, *routing)
     return (in_grad, w_in_grad, w_out_grad, router_grad.T)
 
 

time: 29.5 us -> 29.2 us (0.990)
  Pallas kernels: 28.7 us -> 28.3 us
    pallas_call x1, Pallas kernels: 3.03 us -> 2.68 us  [fused(): pl.pallas_call(functools.partial(finish_kernel, window), out_shape=(jax.S...]
where the time goes in v5:
time: 29.2 us; the launch traced here: 29 us
  Pallas kernels  28.3 us (97%)
  between operations  0.64 us (2%)
    pallas_call x1, Pallas kernels, fused(): pl.pallas_call(functools.partial(fused_kernel, window, groups), out_shape...  25.7 us
    pallas_call x1, Pallas kernels, fused(): pl.pallas_call(functools.partial(finish_kernel, window), out_shape=(jax.S...  2.68 us

profile of v5, /device:TPU:0, one launch (start us, length us, event | category | flops | bytes accessed | tf_op | source)
XLA Modules:
  0.0 29.0 jit_solution(5975004786771843868)
XLA Ops:
  0.6 25.7 %shard_map.111 = (bf16[1024,512]{1,0:T(8,128)(2,1)}, bf16[512,1024]{1,0:T(8,128)(2,1)}, bf16[4,16,128]{2,1,0:T(8,128)(2,1)}, f32[32,256]{1,0:T(8,128)}) custom-call(bf16[128,1024]{1,0:T(8,128)(2,1)} %tokens_hbm.1, bf16[128,1024]{1,0:T(8,128)(2,1)} %out_grad_hbm.1, bf16[32,256]{1,0:T(8,128)(2,1)} %bitcast.5, bf16[1,1024,512]{2,1,0:T(8,128)(2,1)} %w_in_hbm.1, ...), custom_call_target="tpu_custom_call" | custom-call | tf_op jit(solution)/shard_map/pallas_call | solution.py:604
  26.3 2.7 %shard_map.112 = (bf16[128,1024]{1,0:T(8,128)(2,1)}, bf16[1,1024,512]{2,1,0:T(8,128)(2,1)}, bf16[1,512,1024]{2,1,0:T(8,128)(2,1)}, f32[32,256]{1,0:T(8,128)}) custom-call(bf16[1024,512]{1,0:T(8,128)(2,1)} %get-tuple-element.12.g1_hbm, bf16[512,1024]{1,0:T(8,128)(2,1)} %get-tuple-element.13.g2_hbm, bf16[4,16,128]{2,1,0:T(8,128)(2,1)} %get-tuple-element.14.returned_hbm, ...), custom_call_target="tpu_custom_call" | custom-call | tf_op jit(solution)/shard_map/pallas_call | solution.py:658

commit v6 on v5

--- a/solution.py
+++ b/solution.py
@@ -284,8 +284,9 @@
     x_pack,
     dy_pack,
     xs,
-    gv_send,
-    gv_recv,
+    gaps,
+    diff_send,
+    diff_recv,
     gg,
     rp_send,
     rp_recv,
@@ -300,7 +301,8 @@
     ws,
     xps,
     dps,
-    gvs,
+    gps,
+    dfs,
     ggs,
     rps,
     rgs,
@@ -357,12 +359,6 @@
         every = dst.at[pl.ds(0, plane - 1)]
         return remote(every, every, sems, in_plane(q_up(1)))
 
-    barrier = pltpu.get_barrier_semaphore()
-    for d in range(1, window):
-        pl.semaphore_signal(barrier, inc=1, device_id=z_up(d), device_id_type=MESH)
-    for d in range(1, plane):
-        pl.semaphore_signal(barrier, inc=1, device_id=in_plane(q_up(d)), device_id_type=MESH)
-
     loads = [
         pltpu.make_async_copy(src, dst, load_sems.at[i])
         for i, (src, dst) in enumerate(
@@ -378,7 +374,15 @@
             ]
         )
     ]
-    for load in loads:
+    for load in loads[:5]:
+        load.start()
+    barrier = pltpu.get_barrier_semaphore()
+    for d in range(1, window):
+        pl.semaphore_signal(barrier, inc=1, device_id=z_up(d), device_id_type=MESH)
+    for d in range(1, plane):
+        pl.semaphore_signal(barrier, inc=1, device_id=in_plane(q_up(d)), device_id_type=MESH)
+
+    for load in loads[5:]:
         load.start()
 
     depth_f = (2 * chunks + 2) * rows
@@ -440,22 +444,22 @@
     loads[5].wait()
     w_all = along_z(lambda d: w_recv.at[0], w_recv, ws, z_up)
     z_all.wait_recv()
-    gathered = contract(
-        gather, z_recv[...].reshape(window * message, LANES), 1, 0
-    ).astype(BF16)
+    arrived = z_recv[...].reshape(window * message, LANES)
+    x_blocks = (side + 1) * 16
+    gathered = contract(gather[:x_blocks], arrived, 1, 0).astype(BF16)
     for c in range(side + 1):
         x_pack[q, :, c * LANES : (c + 1) * LANES] = gathered[c * 16 : (c + 1) * 16]
+    xp_all = all_plane(lambda p: x_pack.at[q], x_pack, xps)
+    gathered = contract(gather[x_blocks:], arrived, 1, 0).astype(BF16)
     for c in range(side):
-        first = (side + 1 + c) * 16
-        dy_pack[q, :, c * LANES : (c + 1) * LANES] = gathered[first : first + 16]
+        dy_pack[q, :, c * LANES : (c + 1) * LANES] = gathered[c * 16 : (c + 1) * 16]
+    dp_all = all_plane(lambda p: dy_pack.at[q], dy_pack, dps)
 
     def unfolded(block):
         return jnp.concatenate(
             [block[:, :rows, :half], block[:, rows:, :half]], axis=2
         ).reshape(plane * rows, width)
 
-    xp_all = all_plane(lambda p: x_pack.at[q], x_pack, xps)
-    dp_all = all_plane(lambda p: dy_pack.at[q], dy_pack, dps)
     z_all.wait_send()
     w_all.wait()
     router = w_recv[...].reshape(window * columns, depth)
@@ -470,12 +474,13 @@
     hot = one_hot(info[:, 0:1] == column_id) - one_hot(info[:, 1:2] == column_id)
     sign = info[:, 2:3]
     gap_part = jnp.sum(contract(x_part, router, 1, 1) * hot, axis=1, keepdims=True)
+    gap_row = jnp.sum(jnp.where(eye, gap_part, 0.0), axis=0, keepdims=True)
+    gaps[q] = jnp.broadcast_to(gap_row, (rows, LANES))
+    gap_all = all_plane(lambda p: gaps.at[q], gaps, gps)
     row_diff = contract(hot.astype(BF16), router, 1, 0)
-    gap_row = jnp.sum(jnp.where(eye, gap_part, 0.0), axis=0, keepdims=True)
-    gv_send[:, :, :depth] = row_diff.reshape(plane, rows, depth)
-    gv_send[:, :, depth:] = jnp.broadcast_to(gap_row[None], (plane, rows, LANES))
-    gv_recv[q] = gv_send[q]
-    gv_all = all_plane(lambda p: gv_send.at[p], gv_recv, gvs)
+    diff_send[...] = row_diff.reshape(plane, rows, depth)
+    diff_recv[q] = diff_send[q]
+    diff_all = all_plane(lambda p: diff_send.at[p], diff_recv, dfs)
 
     loads[6].wait()
     pre_act = contract(x_rows, w1[...], 1, 0)
@@ -489,8 +494,8 @@
     gg[q] = jnp.broadcast_to(gate_row, (rows, LANES))
     gg_all = all_plane(lambda p: gg.at[q], gg, ggs)
 
-    gv_all.wait_recv()
-    gap_sum = jnp.sum(gv_recv[:, 0:1, depth:], axis=0)
+    gap_all.wait_recv()
+    gap_sum = jnp.sum(gaps[:, 0:1, :], axis=0)
     gap = jnp.sum(jnp.where(eye, gap_sum, 0.0), axis=1, keepdims=True)
     combine_first = jax.nn.sigmoid(gap)
     combine_second = jax.nn.sigmoid(-gap)
@@ -522,11 +527,12 @@
         rg_send[d] = router_part[d * columns : (d + 1) * columns].astype(BF16)
     rg_all = along_z(lambda d: rg_send.at[d], rg_recv, rgs, z_down)
 
+    diff_all.wait_recv()
     diffs = []
     for part in range(groups):
-        diff = gv_recv[part, :, :depth]
+        diff = diff_recv[part]
         for other in range(1, SPLIT):
-            diff = diff + gv_recv[other * groups + part, :, :depth]
+            diff = diff + diff_recv[other * groups + part]
         diffs.append(diff)
     own_coef = coef_ref[pl.ds(pl.multiple_of(q * rows, rows), rows), 0:1]
     router_rows = own_coef * jnp.concatenate(diffs, axis=1)
@@ -551,7 +557,7 @@
             stores[-1].start()
 
     weight_grad(x_rows, pre_grad, g1, g1_out)
-    for sent in (xp_all, dp_all, gv_all, gg_all):
+    for sent in (xp_all, dp_all, gap_all, diff_all, gg_all):
         sent.wait_send()
     halves = []
     for h in range(2):
@@ -628,8 +634,9 @@
             pltpu.VMEM((plane, 16, width // 2 + LANES), BF16),
             pltpu.VMEM((plane, 16, width // 2), BF16),
             pltpu.VMEM((plane * rows, width), BF16),
-            pltpu.VMEM((plane, rows, depth + LANES), F32),
-            pltpu.VMEM((plane, rows, depth + LANES), F32),
+            pltpu.VMEM((plane, rows, LANES), F32),
+            pltpu.VMEM((plane, rows, depth), F32),
+            pltpu.VMEM((plane, rows, depth), F32),
             pltpu.VMEM((plane, rows, LANES), F32),
             pltpu.VMEM((2, plane, 16, width // 4), BF16),
             pltpu.VMEM((2, plane, 16, width // 4), BF16),
@@ -641,7 +648,7 @@
             dma((8,)),
             dma((10,)),
         ]
-        + [dma((2,))] * 6
+        + [dma((2,))] * 7
         + [dma((2, 2))]
         + [dma((2,))] * 2,
         compiler_params=pltpu.CompilerParams(

time: 29.2 us -> 28.9 us (0.990)
    pallas_call x1, Pallas kernels: 25.7 us -> 25.4 us  [fused(): pl.pallas_call(functools.partial(fused_kernel, window, groups), out_shape...]
where the time goes in v6:
time: 28.9 us; the launch traced here: 28.7 us
  Pallas kernels  28.1 us (97%)
  between operations  0.64 us (2%)
    pallas_call x1, Pallas kernels, fused(): pl.pallas_call(functools.partial(fused_kernel, window, groups), out_shape...  25.4 us
    pallas_call x1, Pallas kernels, fused(): pl.pallas_call(functools.partial(finish_kernel, window), out_shape=(jax.S...  2.69 us

profile of v6, /device:TPU:0, one launch (start us, length us, event | category | flops | bytes accessed | tf_op | source)
XLA Modules:
  0.0 28.7 jit_solution(10468476806949764037)
XLA Ops:
  0.6 25.4 %shard_map.111 = (bf16[1024,512]{1,0:T(8,128)(2,1)}, bf16[512,1024]{1,0:T(8,128)(2,1)}, bf16[4,16,128]{2,1,0:T(8,128)(2,1)}, f32[32,256]{1,0:T(8,128)}) custom-call(bf16[128,1024]{1,0:T(8,128)(2,1)} %tokens_hbm.1, bf16[128,1024]{1,0:T(8,128)(2,1)} %out_grad_hbm.1, bf16[32,256]{1,0:T(8,128)(2,1)} %bitcast.5, bf16[1,1024,512]{2,1,0:T(8,128)(2,1)} %w_in_hbm.1, ...), custom_call_target="tpu_custom_call" | custom-call | tf_op jit(solution)/shard_map/pallas_call | solution.py:610
  26.0 2.7 %shard_map.112 = (bf16[128,1024]{1,0:T(8,128)(2,1)}, bf16[1,1024,512]{2,1,0:T(8,128)(2,1)}, bf16[1,512,1024]{2,1,0:T(8,128)(2,1)}, f32[32,256]{1,0:T(8,128)}) custom-call(bf16[1024,512]{1,0:T(8,128)(2,1)} %get-tuple-element.12.g1_hbm, bf16[512,1024]{1,0:T(8,128)(2,1)} %get-tuple-element.13.g2_hbm, bf16[4,16,128]{2,1,0:T(8,128)(2,1)} %get-tuple-element.14.returned_hbm, ...), custom_call_target="tpu_custom_call" | custom-call | tf_op jit(solution)/shard_map/pallas_call | solution.py:665

commit v7 on v6

--- a/solution.py
+++ b/solution.py
@@ -195,12 +195,12 @@
     parts = 4
     loads, stores = [], []
     for src, staged, dst, pieces in (
+        (g1_hbm, g1, w_in_grad_hbm.at[0], parts),
         (ids_hbm, ids_ref, None, 1),
         (slots_hbm, slots_ref, None, 1),
         (keep_hbm, keep_ref, None, 1),
         (returned_hbm, returned_ref, None, 1),
         (router_hbm, router_grad, router_grad_hbm, 1),
-        (g1_hbm, g1, w_in_grad_hbm.at[0], parts),
         (g2_hbm, g2, w_out_grad_hbm.at[0], parts),
     ):
         step = src.shape[0] // pieces
@@ -231,11 +231,14 @@
     source = ((row >> 1) & (window - 1)) * 16 + (row >> 3) * CAP + (row & 1)
     unfold = one_hot(iota((back, back), 1) == source).astype(BF16)
     z = lax.axis_index("expert") // SPLIT
-    for load in loads[:3]:
+    for load, store in zip(loads[:parts], stores):
+        load.wait()
+        store.start()
+    for load in loads[parts : parts + 3]:
         load.wait()
     places = choice_places(LANES, z, window, ids_ref, slots_ref, keep_ref)
     spread_back = jnp.transpose(places[0] + places[1]).astype(BF16)
-    loads[3].wait()
+    loads[parts + 3].wait()
     flat = contract(unfold, returned_ref[...].reshape(back, LANES), 1, 0)
     returned = jnp.concatenate(
         [flat[c * rows : (c + 1) * rows] for c in range(chunks)], axis=1
@@ -243,7 +246,7 @@
     returned = jnp.concatenate(
         [returned, jnp.zeros((LANES - rows, chunks * LANES), F32)], axis=0
     ).astype(BF16)
-    for load, store in zip(loads[4:], stores):
+    for load, store in zip(loads[parts + 4 :], stores[parts:]):
         load.wait()
         store.start()
     in_grad[...] = contract(spread_back, returned, 1, 0).astype(BF16)

time: 28.9 us -> 28.9 us (level)
  no operation moved by 1% of the time
where the time goes in v7:
time: 28.9 us; the launch traced here: 28.7 us
  Pallas kernels  28.1 us (97%)
  between operations  0.64 us (2%)
    pallas_call x1, Pallas kernels, fused(): pl.pallas_call(functools.partial(fused_kernel, window, groups), out_shape...  25.4 us
    pallas_call x1, Pallas kernels, fused(): pl.pallas_call(functools.partial(finish_kernel, window), out_shape=(jax.S...  2.69 us

profile of v7, /device:TPU:0, one launch (start us, length us, event | category | flops | bytes accessed | tf_op | source)
XLA Modules:
  0.0 28.7 jit_solution(11884959194976645014)
XLA Ops:
  0.6 25.4 %shard_map.111 = (bf16[1024,512]{1,0:T(8,128)(2,1)}, bf16[512,1024]{1,0:T(8,128)(2,1)}, bf16[4,16,128]{2,1,0:T(8,128)(2,1)}, f32[32,256]{1,0:T(8,128)}) custom-call(bf16[128,1024]{1,0:T(8,128)(2,1)} %tokens_hbm.1, bf16[128,1024]{1,0:T(8,128)(2,1)} %out_grad_hbm.1, bf16[32,256]{1,0:T(8,128)(2,1)} %bitcast.5, bf16[1,1024,512]{2,1,0:T(8,128)(2,1)} %w_in_hbm.1, ...), custom_call_target="tpu_custom_call" | custom-call | tf_op jit(solution)/shard_map/pallas_call | solution.py:613
  26.0 2.7 %shard_map.112 = (bf16[128,1024]{1,0:T(8,128)(2,1)}, bf16[1,1024,512]{2,1,0:T(8,128)(2,1)}, bf16[1,512,1024]{2,1,0:T(8,128)(2,1)}, f32[32,256]{1,0:T(8,128)}) custom-call(bf16[1024,512]{1,0:T(8,128)(2,1)} %get-tuple-element.12.g1_hbm, bf16[512,1024]{1,0:T(8,128)(2,1)} %get-tuple-element.13.g2_hbm, bf16[4,16,128]{2,1,0:T(8,128)(2,1)} %get-tuple-element.14.returned_hbm, ...), custom_call_target="tpu_custom_call" | custom-call | tf_op jit(solution)/shard_map/pallas_call | solution.py:668
